TPU v7x, 32 devices: a whole 2x2x4 slice. The times are simulated.
32 devices in a mesh: dom: 4 (over z), blk: 8 (over y, x, core).
Axes of the slice: x: 2, y: 2, z: 4, core: 2. Of those that a mesh axis runs over, the one named last changes fastest.
Arguments:
- features_domain: bfloat16 [24576, 1152], P(('dom', 'blk')), may hold values from -6 to 6
- arrival: int32 [24576], P(('dom', 'blk')), may hold values from 0 to 767, as said below
- positions: float32 [24576, 3], P(('dom', 'blk')), may hold values from 0 to 768, as said below
- species: int32 [24576], P(('dom', 'blk')), may hold values from 0 to 88
- block_count: int32 [384], P(('dom', 'blk')), may hold values from 16 to 64, as said below
- pair_block: int32 [384, 3], P(('dom', 'blk')), may hold values from -1 to 383, as said below
- radial_weights: float32 [8, 7, 128], replicated, may hold values from -0.75 to 0.75
- species_weights: float32 [89, 3, 128], replicated, may hold values from -1 to 1
- mix_weight: bfloat16 [128, 128], replicated, may hold values from -0.5 to 0.5
- self_weight: bfloat16 [128, 128], replicated, may hold values from -0.5 to 0.5
- readout: float32 [128], replicated, may hold values from -0.5 to 0.5
Outputs:
- atom_energy: float32 [24576], P(('dom', 'blk'))
- forces: float32 [24576, 3], P(('dom', 'blk'))
- new_features: bfloat16 [24576, 128], P(('dom', 'blk'))
Inputs may be any that keep to these rules, and one draw needn't show every extreme that they name: `arrival`: on each device of dom+blk its 768 entries are a permutation of 0 to 767. `pair_block`: entry [b, 0] is b - 1 or -1, entry [b, 1] is b, entry [b, 2] is b + 1 or -1; the lists are symmetric: [b, 2] is b + 1 exactly when [b + 1, 0] is b. The first block has no predecessor and the last no successor. `block_count`: the live atoms of a block are its first slots. `positions`: atoms of blocks that are not paired lie a distance of 1 or more apart.
All inputs are finite; a program needn't handle non-finite values.
Results may differ from a plain program's by a relative error of at most 0.015.
Values may be sent and summed in bfloat16 or wider, within the bound.
No kernel may reach another device: no remote copies, remote signals or barrier semaphores. Data moves between devices by JAX's collectives and lax.ppermute only.
A program may use at most 64 MiB of HBM per device.

v0:
```python
import math

import jax
import jax.numpy as jnp
import numpy as np
from jax import lax
from jax.sharding import PartitionSpec as P

BLOCK = 64


ROOT_THREE = math.sqrt(3.0)
DOT_PATH = np.array([0, 5, 5, 5, 6, 6, 6, 6, 6])
CARRY_PATH = np.array([3, 3, 3, 4, 4, 4, 4, 4])


def extended(block, sides, width):
    for axis, dim in sides:
        count = lax.axis_size(axis)
        forward = [(i, i + 1) for i in range(count - 1)]
        backward = [(target, source) for source, target in forward]
        low = lax.ppermute(
            lax.slice_in_dim(block, block.shape[dim] - width, None, axis=dim), axis, forward
        )
        high = lax.ppermute(lax.slice_in_dim(block, 0, width, axis=dim), axis, backward)
        block = jnp.concatenate([low, block, high], axis=dim)
    return block


def harmonics(delta_x, delta_y, delta_z):
    return jnp.stack(
        [
            jnp.ones_like(delta_x),
            delta_x,
            delta_y,
            delta_z,
            ROOT_THREE * delta_x * delta_y,
            ROOT_THREE * delta_y * delta_z,
            0.5 * (2.0 * delta_z * delta_z - delta_x * delta_x - delta_y * delta_y),
            ROOT_THREE * delta_z * delta_x,
            0.5 * ROOT_THREE * (delta_x * delta_x - delta_y * delta_y),
        ]
    )


def pair_mask(pair_row, block_rows):
    columns = jnp.arange(3 * block_rows, dtype=jnp.int32)
    listed = (pair_row >= 0).astype(jnp.float32)
    slot_mask = jnp.where(
        columns < block_rows, listed[0], jnp.where(columns < 2 * block_rows, listed[1], listed[2])
    )
    targets = jnp.arange(block_rows, dtype=jnp.int32)[:, None] + block_rows
    distinct = (targets != columns[None, :]).astype(jnp.float32)
    return slot_mask[None, :] * distinct


def edge_factors(window_pos, pair_keep, basis_count):
    block_rows = pair_keep.shape[0]
    coords = window_pos.T
    centre = coords[:, block_rows : 2 * block_rows]
    delta_x = coords[0][None, :] - centre[0][:, None]
    delta_y = coords[1][None, :] - centre[1][:, None]
    delta_z = coords[2][None, :] - centre[2][:, None]
    spread = delta_x * delta_x + delta_y * delta_y + delta_z * delta_z
    envelope = jnp.maximum(1.0 - spread, 0.0) ** 3 * pair_keep
    orders = jnp.arange(basis_count, dtype=jnp.float32) * math.pi
    radial = envelope[None] * jnp.cos(orders[:, None, None] * spread[None])
    return (radial[:, None] * harmonics(delta_x, delta_y, delta_z)[None]).astype(jnp.bfloat16)


def feature_terms(window_feat, radial_weights):
    values = window_feat.astype(jnp.float32)
    dot_terms = (radial_weights[:, None, DOT_PATH, :] * values[None]).astype(jnp.bfloat16)
    lift_terms = (radial_weights[:, None, 1:3, :] * values[None, :, 0:1, :]).astype(jnp.bfloat16)
    carry_terms = (radial_weights[:, None, CARRY_PATH, :] * values[None, :, 1:, :]).astype(
        jnp.bfloat16
    )
    return (dot_terms, lift_terms, carry_terms)


def block_messages(edges, dot_terms, lift_terms, carry_terms):
    scalar = jnp.einsum("nyij,njyc->ic", edges, dot_terms, preferred_element_type=jnp.float32)
    first_order = jnp.einsum(
        "nmij,njc->mic", edges[:, 1:4], lift_terms[:, :, 0], preferred_element_type=jnp.float32
    )
    second = jnp.einsum(
        "nmij,njc->mic", edges[:, 4:9], lift_terms[:, :, 1], preferred_element_type=jnp.float32
    )
    carried = jnp.einsum(
        "nij,njyc->yic", edges[:, 0], carry_terms, preferred_element_type=jnp.float32
    )
    return jnp.concatenate(
        [scalar[None], first_order + carried[0:3], second + carried[3:8]], axis=0
    )


def atom_outputs(message_rows, gain_rows, self_part, live_rows, mix_weight, self_weight, readout):
    squares = message_rows * message_rows
    basis_rows = (
        message_rows[0]
        + gain_rows[:, 0] * squares[0]
        + gain_rows[:, 1] * jnp.sum(squares[1:4], axis=0)
        + gain_rows[:, 2] * jnp.sum(squares[4:9], axis=0)
    )
    rounded = basis_rows.astype(jnp.bfloat16)
    mixed_rows = jnp.dot(rounded, mix_weight, preferred_element_type=jnp.float32) + jnp.dot(
        self_part, self_weight, preferred_element_type=jnp.float32
    )
    energy = live_rows * jnp.sum(readout[None, :] * jax.nn.silu(mixed_rows), axis=1)
    return (energy, (mixed_rows * live_rows[:, None]).astype(jnp.bfloat16))


def block_outputs(
    window_pos,
    window_feat,
    pair_row,
    gain_rows,
    live_rows,
    radial_weights,
    mix_weight,
    self_weight,
    readout,
):
    block_rows = gain_rows.shape[0]
    pair_keep = pair_mask(pair_row, block_rows)
    dot_terms, lift_terms, carry_terms = feature_terms(window_feat, radial_weights)

    def messages_of(positions_window):
        edges = edge_factors(positions_window, pair_keep, radial_weights.shape[0])
        return block_messages(edges, dot_terms, lift_terms, carry_terms)

    messages, pull_edges = jax.vjp(messages_of, window_pos)
    self_rows = window_feat[block_rows : 2 * block_rows, 0, :]

    def outputs_of(message_rows):
        return atom_outputs(
            message_rows, gain_rows, self_rows, live_rows, mix_weight, self_weight, readout
        )

    energy, pull_atoms, features_out = jax.vjp(outputs_of, messages, has_aux=True)
    (grad_messages,) = pull_atoms(jnp.ones_like(energy))
    (grad_window,) = pull_edges(grad_messages)
    return (energy, features_out, grad_window)


def per_device(
    features_domain,
    arrival,
    positions,
    species,
    block_count,
    pair_block,
    radial_weights,
    species_weights,
    mix_weight,
    self_weight,
    readout,
):
    devices = lax.axis_size(("dom", "blk"))
    atom_rows, feature_cols = features_domain.shape
    piece_rows = atom_rows // devices
    parcels = features_domain.reshape(devices, piece_rows, feature_cols)
    received = lax.all_to_all(parcels, ("dom", "blk"), split_axis=0, concat_axis=0, tiled=True)
    received = received.reshape(atom_rows, feature_cols)
    slot_index = jnp.arange(atom_rows, dtype=jnp.int32)
    live_slots = slot_index % BLOCK < jnp.repeat(block_count, BLOCK, total_repeat_length=atom_rows)
    relaid = jnp.where(
        live_slots[:, None], jnp.take(received, arrival, axis=0), jnp.zeros((), jnp.bfloat16)
    )
    live_float = live_slots.astype(jnp.float32)
    feature_ext = extended(relaid, ((("dom", "blk"), 0),), BLOCK)
    position_ext = extended(positions, ((("dom", "blk"), 0),), BLOCK)
    feature_view = feature_ext.reshape(atom_rows + 2 * BLOCK, 9, -1)
    species_total = species_weights.shape[0]
    one_hot = (species[:, None] == jnp.arange(species_total, dtype=jnp.int32)[None, :]).astype(
        jnp.float32
    )
    gains = jnp.dot(
        one_hot, species_weights.reshape(species_total, -1), precision=lax.Precision.HIGHEST
    ).reshape(atom_rows, 3, -1)
    channels = radial_weights.shape[2]

    def one_block(block_index, loop_state):
        force_ext, energies, new_rows = loop_state
        start_row = block_index * BLOCK
        window_pos = lax.dynamic_slice_in_dim(position_ext, start_row, 3 * BLOCK, 0)
        window_feat = lax.dynamic_slice_in_dim(feature_view, start_row, 3 * BLOCK, 0)
        pair_row = lax.dynamic_index_in_dim(pair_block, block_index, 0, keepdims=False)
        gain_rows = lax.dynamic_slice_in_dim(gains, start_row, BLOCK, 0)
        live_rows = lax.dynamic_slice_in_dim(live_float, start_row, BLOCK, 0)
        energy, features_out, grad_window = block_outputs(
            window_pos,
            window_feat,
            pair_row,
            gain_rows,
            live_rows,
            radial_weights,
            mix_weight,
            self_weight,
            readout,
        )
        current = lax.dynamic_slice_in_dim(force_ext, start_row, 3 * BLOCK, 0)
        force_ext = lax.dynamic_update_slice_in_dim(force_ext, current + grad_window, start_row, 0)
        energies = lax.dynamic_update_slice_in_dim(energies, energy, start_row, 0)
        new_rows = lax.dynamic_update_slice_in_dim(new_rows, features_out, start_row, 0)
        return (force_ext, energies, new_rows)

    initial = (
        jnp.zeros((atom_rows + 2 * BLOCK, 3), jnp.float32),
        jnp.zeros((atom_rows,), jnp.float32),
        jnp.zeros((atom_rows, channels), jnp.bfloat16),
    )
    force_ext, energies, new_rows = lax.fori_loop(0, atom_rows // BLOCK, one_block, initial)
    outgoing = jnp.concatenate([force_ext[:BLOCK], force_ext[atom_rows + BLOCK :]], axis=0)
    incoming = extended(outgoing, ((("dom", "blk"), 0),), BLOCK)
    own_forces = force_ext[BLOCK : atom_rows + BLOCK]
    own_forces = own_forces.at[:BLOCK].add(incoming[:BLOCK])
    own_forces = own_forces.at[atom_rows - BLOCK :].add(incoming[3 * BLOCK :])
    return (energies, -own_forces, new_rows)


def solution(mesh):
    placed = (
        P(("dom", "blk"), None),
        P(("dom", "blk")),
        P(("dom", "blk"), None),
        P(("dom", "blk")),
        P(("dom", "blk")),
        P(("dom", "blk"), None),
        P(),
        P(),
        P(),
        P(),
        P(),
    )
    return jax.shard_map(
        per_device,
        mesh=mesh,
        in_specs=placed,
        out_specs=(P(("dom", "blk")), P(("dom", "blk"), None), P(("dom", "blk"), None)),
        check_vma=False,
    )
```

profile of v0, /device:TPU:4, one launch (start us, length us, event | category | flops | bytes accessed | tf_op | source)
XLA Modules:
  0.0 513.6 jit_solution(2936951647407351133)
XLA Ops:
  0.7 6.1 %all-to-all-start = ((bf16[32,24,1152]{2,1,0:T(8,128)(2,1)}), bf16[32,24,1152]{2,1,0:T(8,128)(2,1)S(1)}, u32[]{:S(2)}, u32[]{:S(2)}) async-start(bf16[32,24,1152]{2,1,0:T(8,128)(2,1)} %bitcast.390), calls=%async_computation | async-start | bytes 3538944 | tf_op jit(solution)/shard_map/all_to_all | solution.py:163
  9.5 4.4 collective-permute-start.1
  15.7 4.5 fusion.111
  20.8 3.8 fusion.115
  24.6 23.6 %all-to-all-done = bf16[32,24,1152]{2,1,0:T(8,128)(2,1)S(1)} async-done(((bf16[32,24,1152]{2,1,0:T(8,128)(2,1)}), bf16[32,24,1152]{2,1,0:T(8,128)(2,1)S(1)}, u32[]{:S(2)}, u32[]{:S(2)}) %all-to-all-start) | async-done | bytes 1769504 | tf_op jit(solution)/shard_map/all_to_all | solution.py:163
  48.2 2.9 gather_fusion.2
  54.2 4.7 collective-permute-start.3
  62.9 2.9 copy.29
  65.8 2.4 copy.32
  70.1 433.1 %while.21 = (s32[]{:T(128)}, f32[896,3]{0,1:T(4,128)}, f32[768]{0:T(1024)}, bf16[768,128]{1,0:T(8,128)(2,1)}, f32[896,3]{0,1:T(4,128)S(1)}, /*index=5*/s32[12,3]...) while((s32[]{:T(128)}, f32[896,3]{0,1:T(4,128)}, ...), condition=%wide.region_14.15_spmd.clone, body=%wide.region_0.14_spmd.sunk.clone.sunk | while | flops 1296982656 | bytes 45422888 | solution.py:213
  98.1 3.0 fusion.190
  101.1 2.2 fusion.191
  134.1 3.0 fusion.190
  137.2 2.2 fusion.191
  170.3 3.0 fusion.190
  173.3 2.2 fusion.191
  206.3 3.0 fusion.190
  209.4 2.2 fusion.191
  242.5 3.0 fusion.190
  245.6 2.2 fusion.191
  278.6 3.0 fusion.190
  281.6 2.2 fusion.191
  314.7 3.0 fusion.190
  350.8 3.0 fusion.190
  353.8 2.2 fusion.191
  386.9 3.0 fusion.190
  390.0 2.2 fusion.191
  423.0 3.0 fusion.190
  459.1 3.0 fusion.190
  495.1 3.0 fusion.190
  504.0 2.8 collective-permute-start.4
  507.6 3.8 collective-permute-start.5
  (1489 shorter events, 389.3 us)
Async XLA Ops:
  0.6 13.3 %copy-start.22 = (f32[89,3,128]{2,0,1:T(8,128)S(1)}, f32[89,3,128]{2,0,1:T(8,128)}, u32[]{:S(2)}) copy-start(f32[89,3,128]{2,0,1:T(8,128)} %param.30) | copy-start | bytes 410116
  0.7 14.2 %copy-start.33 = (s32[768]{0:T(1024)S(1)}, s32[768]{0:T(1024)}, u32[]{:S(2)}) copy-start(s32[768]{0:T(1024)} %param.24) | copy-start | bytes 9220
  0.7 14.2 %copy-start.27 = (s32[12]{0:T(128)S(1)}, s32[12]{0:T(128)}, u32[]{:S(2)}) copy-start(s32[12]{0:T(128)} %param.27) | copy-start | bytes 148
  0.7 14.9 %copy-start.34 = (s32[6,128]{1,0:T(8,128)S(1)}, s32[6,128]{1,0:T(8,128)}, u32[]{:S(2)}) copy-start(s32[6,128]{1,0:T(8,128)} %constant.303.clone.1) | copy-start | bytes 9220
  0.7 47.5 %all-to-all-start = ((bf16[32,24,1152]{2,1,0:T(8,128)(2,1)}), bf16[32,24,1152]{2,1,0:T(8,128)(2,1)S(1)}, u32[]{:S(2)}, u32[]{:S(2)}) async-start(bf16[32,24,1152]{2,1,0:T(8,128)(2,1)} %bitcast.390), calls=%async_computation | async-start | bytes 3538944 | tf_op jit(solution)/shard_map/all_to_all | solution.py:163
  7.5 53.2 %collective-permute-start = (f32[64,3]{0,1:T(4,128)}, f32[64,3]{0,1:T(4,128)}, u32[]{:S(2)}, u32[]{:S(2)}) collective-permute-start(f32[64,3]{0,1:T(4,128)} %get-tuple-element.463), channel_id=1, source_target_pairs={{0,1},{1,2},{2,3},{3,4},{4,5},{5,6},{6,7},{7,8},{8,9},{9,10},{10,1... | collective-permute-start | bytes 2312 | tf_op jit(solution)/shard_map/ppermute | solution.py:22
  9.5 51.1 %collective-permute-start.1 = (f32[64,3]{0,1:T(4,128)}, f32[64,3]{0,1:T(4,128)}, u32[]{:S(2)}, u32[]{:S(2)}) collective-permute-start(f32[64,3]{0,1:T(4,128)} %get-tuple-element.464), channel_id=1, source_target_pairs={{1,0},{2,1},{3,2},{4,3},{5,4},{6,5},{7,6},{8,7},{9,8},{10,9},{11,1... | collective-permute-start | bytes 2312 | tf_op jit(solution)/shard_map/ppermute | solution.py:25
  52.3 9.1 %collective-permute-start.2 = (bf16[64,1152]{1,0:T(8,128)(2,1)S(1)}, bf16[64,1152]{1,0:T(8,128)(2,1)S(1)}, u32[]{:S(2)}, u32[]{:S(2)}) collective-permute-start(bf16[64,1152]{1,0:T(8,128)(2,1)S(1)} %get-tuple-element.459), channel_id=1, source_target_pairs={{0,1},{1,2},{2,3},{3,4},{4,5},{5,6},{6,7},{7,8},{8,9},{9,10},{10,1... | collective-permute-start | bytes 442376 | tf_op jit(solution)/shard_map/ppermute | solution.py:22
  54.2 7.2 %collective-permute-start.3 = (bf16[64,1152]{1,0:T(8,128)(2,1)S(1)}, bf16[64,1152]{1,0:T(8,128)(2,1)S(1)}, u32[]{:S(2)}, u32[]{:S(2)}) collective-permute-start(bf16[64,1152]{1,0:T(8,128)(2,1)S(1)} %get-tuple-element.460), channel_id=1, source_target_pairs={{1,0},{2,1},{3,2},{4,3},{5,4},{6,5},{7,6},{8,7},{9,8},{10,9},{11,1... | collective-permute-start | bytes 442376 | tf_op jit(solution)/shard_map/ppermute | solution.py:25
  86.4 9.5 %copy-start.3 = (f32[192,8,128]{2,0,1:T(8,128)S(1)}, f32[192,8,128]{2,0,1:T(8,128)}, u32[]{:S(2)}) copy-start(f32[192,8,128]{2,0,1:T(8,128)} %slice.481) | copy-start | bytes 2359300 | tf_op jit(solution)/shard_map/while
  122.5 9.5 %copy-start.3 = (f32[192,8,128]{2,0,1:T(8,128)S(1)}, f32[192,8,128]{2,0,1:T(8,128)}, u32[]{:S(2)}) copy-start(f32[192,8,128]{2,0,1:T(8,128)} %slice.481) | copy-start | bytes 2359300 | tf_op jit(solution)/shard_map/while
  134.1 8.3 %copy-start.26 = (f32[896,3]{0,1:T(4,128)S(1)}, f32[896,3]{0,1:T(4,128)}, u32[]{:S(2)}) copy-start(f32[896,3]{0,1:T(4,128)} %copy-done.25) | copy-start | bytes 32260 | tf_op jit(solution)/shard_map/while
  134.1 8.3 %copy-start.29 = (s32[12,3]{0,1:T(4,128)S(1)}, s32[12,3]{0,1:T(4,128)}, u32[]{:S(2)}) copy-start(s32[12,3]{0,1:T(4,128)} %get-tuple-element.721) | copy-start | bytes 436 | tf_op jit(solution)/shard_map/while
  134.1 8.3 %copy-start.36 = (s32[8]{0:T(128)S(1)}, s32[8]{0:T(128)}, u32[]{:S(2)}) copy-start(s32[8]{0:T(128)} %get-tuple-element.746) | copy-start | bytes 100 | tf_op jit(solution)/shard_map/while
  158.6 9.5 %copy-start.3 = (f32[192,8,128]{2,0,1:T(8,128)S(1)}, f32[192,8,128]{2,0,1:T(8,128)}, u32[]{:S(2)}) copy-start(f32[192,8,128]{2,0,1:T(8,128)} %slice.481) | copy-start | bytes 2359300 | tf_op jit(solution)/shard_map/while
  194.7 9.5 %copy-start.3 = (f32[192,8,128]{2,0,1:T(8,128)S(1)}, f32[192,8,128]{2,0,1:T(8,128)}, u32[]{:S(2)}) copy-start(f32[192,8,128]{2,0,1:T(8,128)} %slice.481) | copy-start | bytes 2359300 | tf_op jit(solution)/shard_map/while
  206.3 8.3 %copy-start.26 = (f32[896,3]{0,1:T(4,128)S(1)}, f32[896,3]{0,1:T(4,128)}, u32[]{:S(2)}) copy-start(f32[896,3]{0,1:T(4,128)} %copy-done.25) | copy-start | bytes 32260 | tf_op jit(solution)/shard_map/while
  206.3 8.3 %copy-start.29 = (s32[12,3]{0,1:T(4,128)S(1)}, s32[12,3]{0,1:T(4,128)}, u32[]{:S(2)}) copy-start(s32[12,3]{0,1:T(4,128)} %get-tuple-element.721) | copy-start | bytes 436 | tf_op jit(solution)/shard_map/while
  230.9 9.5 %copy-start.3 = (f32[192,8,128]{2,0,1:T(8,128)S(1)}, f32[192,8,128]{2,0,1:T(8,128)}, u32[]{:S(2)}) copy-start(f32[192,8,128]{2,0,1:T(8,128)} %slice.481) | copy-start | bytes 2359300 | tf_op jit(solution)/shard_map/while
  266.9 9.5 %copy-start.3 = (f32[192,8,128]{2,0,1:T(8,128)S(1)}, f32[192,8,128]{2,0,1:T(8,128)}, u32[]{:S(2)}) copy-start(f32[192,8,128]{2,0,1:T(8,128)} %slice.481) | copy-start | bytes 2359300 | tf_op jit(solution)/shard_map/while
  278.5 8.3 %copy-start.26 = (f32[896,3]{0,1:T(4,128)S(1)}, f32[896,3]{0,1:T(4,128)}, u32[]{:S(2)}) copy-start(f32[896,3]{0,1:T(4,128)} %copy-done.25) | copy-start | bytes 32260 | tf_op jit(solution)/shard_map/while
  278.5 8.3 %copy-start.29 = (s32[12,3]{0,1:T(4,128)S(1)}, s32[12,3]{0,1:T(4,128)}, u32[]{:S(2)}) copy-start(s32[12,3]{0,1:T(4,128)} %get-tuple-element.721) | copy-start | bytes 436 | tf_op jit(solution)/shard_map/while
  303.1 9.5 %copy-start.3 = (f32[192,8,128]{2,0,1:T(8,128)S(1)}, f32[192,8,128]{2,0,1:T(8,128)}, u32[]{:S(2)}) copy-start(f32[192,8,128]{2,0,1:T(8,128)} %slice.481) | copy-start | bytes 2359300 | tf_op jit(solution)/shard_map/while
  339.1 9.5 %copy-start.3 = (f32[192,8,128]{2,0,1:T(8,128)S(1)}, f32[192,8,128]{2,0,1:T(8,128)}, u32[]{:S(2)}) copy-start(f32[192,8,128]{2,0,1:T(8,128)} %slice.481) | copy-start | bytes 2359300 | tf_op jit(solution)/shard_map/while
  350.7 8.3 %copy-start.26 = (f32[896,3]{0,1:T(4,128)S(1)}, f32[896,3]{0,1:T(4,128)}, u32[]{:S(2)}) copy-start(f32[896,3]{0,1:T(4,128)} %copy-done.25) | copy-start | bytes 32260 | tf_op jit(solution)/shard_map/while
  375.3 9.5 %copy-start.3 = (f32[192,8,128]{2,0,1:T(8,128)S(1)}, f32[192,8,128]{2,0,1:T(8,128)}, u32[]{:S(2)}) copy-start(f32[192,8,128]{2,0,1:T(8,128)} %slice.481) | copy-start | bytes 2359300 | tf_op jit(solution)/shard_map/while
  411.3 9.5 %copy-start.3 = (f32[192,8,128]{2,0,1:T(8,128)S(1)}, f32[192,8,128]{2,0,1:T(8,128)}, u32[]{:S(2)}) copy-start(f32[192,8,128]{2,0,1:T(8,128)} %slice.481) | copy-start | bytes 2359300 | tf_op jit(solution)/shard_map/while
  422.9 8.3 %copy-start.26 = (f32[896,3]{0,1:T(4,128)S(1)}, f32[896,3]{0,1:T(4,128)}, u32[]{:S(2)}) copy-start(f32[896,3]{0,1:T(4,128)} %copy-done.25) | copy-start | bytes 32260 | tf_op jit(solution)/shard_map/while
  447.5 9.5 %copy-start.3 = (f32[192,8,128]{2,0,1:T(8,128)S(1)}, f32[192,8,128]{2,0,1:T(8,128)}, u32[]{:S(2)}) copy-start(f32[192,8,128]{2,0,1:T(8,128)} %slice.481) | copy-start | bytes 2359300 | tf_op jit(solution)/shard_map/while
  483.5 9.5 %copy-start.3 = (f32[192,8,128]{2,0,1:T(8,128)S(1)}, f32[192,8,128]{2,0,1:T(8,128)}, u32[]{:S(2)}) copy-start(f32[192,8,128]{2,0,1:T(8,128)} %slice.481) | copy-start | bytes 2359300 | tf_op jit(solution)/shard_map/while
  504.0 7.4 %collective-permute-start.4 = (f32[64,3]{0,1:T(4,128)S(1)}, f32[64,3]{0,1:T(4,128)S(1)}, u32[]{:S(2)}, u32[]{:S(2)}) collective-permute-start(f32[64,3]{0,1:T(4,128)S(1)} %get-tuple-element.462), channel_id=1, source_target_pairs={{0,1},{1,2},{2,3},{3,4},{4,5},{5,6},{6,7},{7,8},{8,9},{9,10},{10,1... | collective-permute-start | bytes 2312 | tf_op jit(solution)/shard_map/ppermute | solution.py:22
  507.6 5.1 collective-permute-start.5
  (334 other events, 1288.2 us)
where the time goes:
time: 522 us; the launch traced here: 514 us
  other arithmetic  198 us (38%)
  matrix products  162 us (31%)
  local copies, waits for them, and re-layouts  95.3 us (18%)
  starting transfers between devices  25.8 us (5%)
  waiting for transfers between devices  24.1 us (5%)
  loops' own time  7.81 us (1%)
    dot_general x24, matrix products, block_messages(): jnp.einsum('nyij,njyc->ic', edges, dot_terms, preferred_element_type=jnp....  50.9 us
    dot_general x24, matrix products, block_messages(): jnp.einsum('nij,njyc->yic', edges[:, 0], carry_terms, preferred_element_t...  36.5 us
    dot_general x24, matrix products, atom_outputs(): jnp.dot(rounded, mix_weight, preferred_element_type=jnp.float32)  30.8 us
    while x708, local copies, waits for them, and re-layouts  29 us
    reduce_sum x12, other arithmetic, edge_factors(): radial = envelope[None] * jnp.cos(orders[:, None, None] * spread[None])  26.3 us
    all_to_all x1, waiting for transfers between devices, per_device(): lax.all_to_all(parcels, ('dom', 'blk'), split_axis=0, concat_axis=0, tile...  23.6 us
    select_n x12, other arithmetic, pair_mask(): jnp.where(columns < block_rows, listed[0], jnp.where(columns < 2 * block_...  22.4 us
    mul x12, other arithmetic, edge_factors(): radial = envelope[None] * jnp.cos(orders[:, None, None] * spread[None])  21 us
  transfers between devices with their start and end apart: 7, of which 2 were waited for; matrix products, arithmetic and copies ran while one was open for 4% of the time, Pallas kernels for 0%

commit v1 on v0

v1 whole, which is shorter than its diff:
```python
import functools
import math

import jax
import jax.numpy as jnp
import numpy as np
from jax import lax
from jax.experimental import pallas as pl
from jax.experimental.pallas import tpu as pltpu
from jax.sharding import PartitionSpec as P

BLOCK = 64
TILE = 2 * BLOCK
WINDOW = 4 * BLOCK
HARM = 9
ROOT_THREE = math.sqrt(3.0)
AXES = ("dom", "blk")
VMEM_BYTES = 56 * 1024 * 1024


def degree(k):
    return 0 if k == 0 else (1 if k < 4 else 2)


def relay_kernel(arrival_ref, received_ref, relaid_ref):
    rows = received_ref.shape[0]
    wanted = jnp.transpose(jnp.broadcast_to(arrival_ref[...], (8, rows)))[:, 0:1]
    source = lax.broadcasted_iota(jnp.int32, (TILE, rows), 1)
    for part in range(rows // TILE):
        here = slice(part * TILE, (part + 1) * TILE)
        chosen = (wanted[here] == source).astype(jnp.float32).astype(jnp.bfloat16)
        relaid_ref[here, :] = jnp.dot(
            chosen, received_ref[...], preferred_element_type=jnp.float32
        ).astype(jnp.bfloat16)


def relay(arrival_live, received):
    rows, cols = received.shape
    return pl.pallas_call(
        relay_kernel,
        out_shape=jax.ShapeDtypeStruct((rows, cols), jnp.bfloat16),
        in_specs=[pl.BlockSpec(memory_space=pltpu.VMEM)] * 2,
        out_specs=pl.BlockSpec(memory_space=pltpu.VMEM),
        compiler_params=pltpu.CompilerParams(vmem_limit_bytes=VMEM_BYTES),
        cost_estimate=pl.CostEstimate(
            flops=2 * rows * rows * cols, bytes_accessed=4 * rows * cols, transcendentals=0
        ),
        name="relay",
    )(arrival_live, received)


def polynomial(square, coefficients):
    total = jnp.full_like(square, coefficients[-1])
    for value in coefficients[-2::-1]:
        total = total * square + value
    return total


SINE = [(-1.0) ** m * math.pi ** (2 * m + 1) / math.factorial(2 * m + 1) for m in range(6)]
COSINE = [(-1.0) ** m * math.pi ** (2 * m) / math.factorial(2 * m) for m in range(7)]


def solid(x, y, z):
    return [
        None,
        x,
        y,
        z,
        ROOT_THREE * x * y,
        ROOT_THREE * y * z,
        z * z - 0.5 * (x * x + y * y),
        ROOT_THREE * z * x,
        (0.5 * ROOT_THREE) * (x * x - y * y),
    ]


def layer_kernel(
    pair_ref,
    rows_ref,
    relaid_ref,
    low_ref,
    high_ref,
    gains_ref,
    radial_ref,
    mix_ref,
    self_ref,
    readout_ref,
    energy_ref,
    force_ref,
    new_ref,
    feat_ref,
    cols_ref,
    edge_ref,
    radial_val_ref,
    radial_der_ref,
    message_ref,
    grad_ref,
    orders,
):
    step = pl.program_id(0)
    atom_rows = relaid_ref.shape[0]
    channels = mix_ref.shape[0]

    @pl.when(step == 0)
    def _():
        feat_ref[0:BLOCK, :] = low_ref[...]
        feat_ref[BLOCK : BLOCK + atom_rows, :] = relaid_ref[...]
        feat_ref[BLOCK + atom_rows :, :] = high_ref[...]
        cols_ref[...] = jnp.transpose(rows_ref[...])
        force_ref[...] = jnp.zeros_like(force_ref)

    base = pl.multiple_of(step * TILE, TILE)
    window = pl.ds(base, WINDOW)
    centre = pl.ds(pl.multiple_of(base + BLOCK, BLOCK), TILE)

    columns = lax.broadcasted_iota(jnp.int32, (BLOCK, WINDOW), 1)
    targets = lax.broadcasted_iota(jnp.int32, (BLOCK, WINDOW), 0)
    keep_parts = []
    for half in range(2):
        listed = [pair_ref[(2 * step + half) * 3 + side] >= 0 for side in range(3)]
        offset = columns - half * BLOCK
        inside = jnp.zeros((BLOCK, WINDOW), jnp.float32)
        for side in range(3):
            member = (offset >= side * BLOCK) & (offset < (side + 1) * BLOCK)
            inside = jnp.where(member, listed[side].astype(jnp.float32), inside)
        keep_parts.append(jnp.where(targets + BLOCK == offset, 0.0, inside))
    keep = jnp.concatenate(keep_parts, axis=0)

    def deltas():
        return [rows_ref[a : a + 1, window] - cols_ref[centre, a : a + 1] for a in range(3)]

    x, y, z = deltas()
    spread = x * x + y * y + z * z
    room = jnp.maximum(1.0 - spread, 0.0)
    squared = room * room * keep
    envelope = squared * room
    slope = -3.0 * squared
    shifted = jnp.minimum(spread, 1.0) - 0.5
    shifted_sq = shifted * shifted
    cosine = -shifted * polynomial(shifted_sq, SINE)
    sine = polynomial(shifted_sq, COSINE)
    twice = 2.0 * cosine
    cos_prev, cos_now = jnp.ones_like(cosine), cosine
    sin_prev, sin_now = jnp.zeros_like(sine), sine
    harm = solid(x, y, z)
    for n in range(orders):
        here = slice(n * TILE, (n + 1) * TILE)
        if n == 0:
            value, change = envelope, slope
        else:
            value = envelope * cos_now
            change = slope * cos_now - (n * math.pi) * (envelope * sin_now)
        radial_val_ref[here, :] = value
        radial_der_ref[here, :] = change
        for k in range(HARM):
            edge = value if k == 0 else value * harm[k]
            edge_ref[k, here, :] = edge.astype(jnp.bfloat16)
        if n >= 1:
            cos_prev, cos_now = cos_now, twice * cos_now - cos_prev
            sin_prev, sin_now = sin_now, twice * sin_now - sin_prev

    def weight(n, path):
        return radial_ref[n * 7 + path : n * 7 + path + 1, :]

    def piece(k):
        return feat_ref[window, k * channels : (k + 1) * channels]

    def path_sum(product, first, path):
        total = None
        for n in range(orders):
            part = product[n * TILE : (n + 1) * TILE, first : first + channels] * weight(n, path)
            total = part if total is None else total + part
        return total

    scalar = None
    for k in range(HARM):
        pairs = jnp.dot(edge_ref[0], piece(k), preferred_element_type=jnp.float32)
        if k == 0:
            scalar = path_sum(pairs, 0, 0)
        else:
            message_ref[k] = path_sum(pairs, 0, 2 + degree(k))
    message_ref[0] = scalar
    for k in range(1, HARM):
        both = jnp.concatenate([piece(k), piece(0)], axis=1)
        pairs = jnp.dot(edge_ref[k], both, preferred_element_type=jnp.float32)
        message_ref[0] += path_sum(pairs, 0, 4 + degree(k))
        message_ref[k] += path_sum(pairs, channels, degree(k))

    own = pl.ds(base, TILE)
    gain = [gains_ref[own, l * channels : (l + 1) * channels] for l in range(3)]
    zero = message_ref[0]
    first = sum(message_ref[k] * message_ref[k] for k in range(1, 4))
    second = sum(message_ref[k] * message_ref[k] for k in range(4, HARM))
    basis = zero + gain[0] * (zero * zero) + gain[1] * first + gain[2] * second
    live = cols_ref[centre, 3:4]
    mixed = jnp.dot(
        basis.astype(jnp.bfloat16), mix_ref[...], preferred_element_type=jnp.float32
    ) + jnp.dot(feat_ref[centre, 0:channels], self_ref[...], preferred_element_type=jnp.float32)
    gate = 1.0 / (1.0 + jnp.exp(-mixed))
    silu = mixed * gate
    readout = readout_ref[...]
    new_ref[own, :] = (live * mixed).astype(jnp.bfloat16)
    energy_ref[0] = jnp.sum(jnp.transpose(live * (readout * silu)), axis=0, keepdims=True)
    mixed_grad = live * readout * (gate * (1.0 + mixed - silu))
    basis_grad = lax.dot_general(
        mixed_grad.astype(jnp.bfloat16),
        mix_ref[...],
        (((1,), (1,)), ((), ())),
        preferred_element_type=jnp.float32,
    )
    grad_ref[0] = (basis_grad * (1.0 + 2.0 * gain[0] * zero)).astype(jnp.bfloat16)
    for k in range(1, HARM):
        grad_ref[k] = (basis_grad * (2.0 * gain[degree(k)]) * message_ref[k]).astype(jnp.bfloat16)

    def against(left, right):
        return lax.dot_general(
            left, right, (((1,), (1,)), ((), ())), preferred_element_type=jnp.float32
        )

    def narrow(n, path):
        return weight(n, path).astype(jnp.bfloat16)

    x, y, z = deltas()
    left = jnp.concatenate(
        [
            jnp.concatenate(
                [grad_ref[k] * narrow(n, 0 if k == 0 else 2 + degree(k)) for k in range(HARM)],
                axis=1,
            )
            for n in range(orders)
        ],
        axis=0,
    )
    cross = against(left, feat_ref[window, :])
    radial_total = sum(
        cross[n * TILE : (n + 1) * TILE] * radial_der_ref[n * TILE : (n + 1) * TILE, :]
        for n in range(orders)
    )
    root_x, root_y, root_z = ROOT_THREE * x, ROOT_THREE * y, ROOT_THREE * z
    slopes = {
        1: {0: None},
        2: {1: None},
        3: {2: None},
        4: {0: root_y, 1: root_x},
        5: {1: root_z, 2: root_y},
        6: {0: -x, 1: -y, 2: 2.0 * z},
        7: {0: root_z, 2: root_x},
        8: {0: root_x, 1: -root_y},
    }
    pull = [None, None, None]
    harm = solid(x, y, z)
    for k in range(1, HARM):
        left = jnp.concatenate(
            [
                jnp.concatenate(
                    [
                        grad_ref[0] * narrow(n, 4 + degree(k)),
                        grad_ref[k] * narrow(n, degree(k)),
                    ],
                    axis=1,
                )
                for n in range(orders)
            ],
            axis=0,
        )
        cross = against(left, jnp.concatenate([piece(k), piece(0)], axis=1))
        along = None
        turned = None
        for n in range(orders):
            here = slice(n * TILE, (n + 1) * TILE)
            part = cross[here]
            one = part * radial_val_ref[here, :]
            two = part * radial_der_ref[here, :]
            along = one if along is None else along + one
            turned = two if turned is None else turned + two
        radial_total = radial_total + turned * harm[k]
        for axis, factor in slopes[k].items():
            term = along if factor is None else along * factor
            pull[axis] = term if pull[axis] is None else pull[axis] + term
    radial_total = 2.0 * radial_total
    columns_out = []
    for axis, delta in enumerate((x, y, z)):
        total = pull[axis] + delta * radial_total
        force_ref[axis : axis + 1, window] -= jnp.sum(total, axis=0, keepdims=True)
        columns_out.append(jnp.sum(total, axis=1, keepdims=True))
    lane = lax.broadcasted_iota(jnp.int32, (TILE, 8), 1)
    packed = jnp.zeros((TILE, 8), jnp.float32)
    for axis in range(3):
        packed = jnp.where(lane == axis, columns_out[axis], packed)
    turned = jnp.transpose(packed)
    padded = jnp.concatenate(
        [jnp.zeros((8, BLOCK), jnp.float32), turned, jnp.zeros((8, BLOCK), jnp.float32)], axis=1
    )
    force_ref[:, window] += padded


def layer(pair, rows, relaid, low, high, gains, radial, mix, self_weight, readout):
    atom_rows, cols = relaid.shape
    channels = mix.shape[0]
    orders = radial.shape[0] // 7
    wide = atom_rows + 2 * BLOCK
    tiles = atom_rows // TILE
    whole = pl.BlockSpec(memory_space=pltpu.VMEM)
    return pl.pallas_call(
        functools.partial(layer_kernel, orders=orders),
        grid=(tiles,),
        out_shape=(
            jax.ShapeDtypeStruct((tiles, 1, TILE), jnp.float32),
            jax.ShapeDtypeStruct((8, wide), jnp.float32),
            jax.ShapeDtypeStruct((atom_rows, channels), jnp.bfloat16),
        ),
        in_specs=[pl.BlockSpec(memory_space=pltpu.SMEM)] + [whole] * 9,
        out_specs=(
            pl.BlockSpec((1, 1, TILE), lambda t: (t, 0, 0)),
            whole,
            whole,
        ),
        scratch_shapes=[
            pltpu.VMEM((wide, cols), jnp.bfloat16),
            pltpu.VMEM((wide, 8), jnp.float32),
            pltpu.VMEM((HARM, orders * TILE, WINDOW), jnp.bfloat16),
            pltpu.VMEM((orders * TILE, WINDOW), jnp.float32),
            pltpu.VMEM((orders * TILE, WINDOW), jnp.float32),
            pltpu.VMEM((HARM, TILE, channels), jnp.float32),
            pltpu.VMEM((HARM, TILE, channels), jnp.bfloat16),
        ],
        compiler_params=pltpu.CompilerParams(vmem_limit_bytes=VMEM_BYTES),
        cost_estimate=pl.CostEstimate(
            flops=tiles * 4 * orders * TILE * WINDOW * channels * 25,
            bytes_accessed=4 * atom_rows * cols,
            transcendentals=0,
        ),
        name="layer",
    )(pair, rows, relaid, low, high, gains, radial, mix, self_weight, readout)


def from_sides(block_low, block_high):
    count = lax.axis_size(AXES)
    forward = [(i, i + 1) for i in range(count - 1)]
    backward = [(target, source) for source, target in forward]
    low = lax.ppermute(block_high, AXES, forward)
    high = lax.ppermute(block_low, AXES, backward)
    return low, high


def per_device(
    features_domain,
    arrival,
    positions,
    species,
    block_count,
    pair_block,
    radial_weights,
    species_weights,
    mix_weight,
    self_weight,
    readout,
):
    devices = lax.axis_size(AXES)
    atom_rows, feature_cols = features_domain.shape
    piece_rows = atom_rows // devices
    parcels = features_domain.reshape(devices, piece_rows, feature_cols)
    received = lax.all_to_all(parcels, AXES, split_axis=0, concat_axis=0, tiled=True)
    received = received.reshape(atom_rows, feature_cols)
    slot_index = jnp.arange(atom_rows, dtype=jnp.int32)
    live = slot_index % BLOCK < jnp.repeat(block_count, BLOCK, total_repeat_length=atom_rows)
    arrival_live = jnp.where(live, arrival, -1).reshape(1, atom_rows)
    coords = positions.T
    low_pos, high_pos = from_sides(coords[:, :BLOCK], coords[:, atom_rows - BLOCK :])
    coords = jnp.concatenate([low_pos, coords, high_pos], axis=1)
    live_row = jnp.pad(live.astype(jnp.float32), (BLOCK, BLOCK)).reshape(1, -1)
    rows = jnp.concatenate([coords, live_row, jnp.zeros((4, coords.shape[1]), jnp.float32)], axis=0)
    species_total = species_weights.shape[0]
    one_hot = (species[:, None] == jnp.arange(species_total, dtype=jnp.int32)[None, :]).astype(
        jnp.float32
    )
    gains = jnp.dot(
        one_hot, species_weights.reshape(species_total, -1), precision=lax.Precision.HIGHEST
    )
    relaid = relay(arrival_live, received)
    low, high = from_sides(relaid[:BLOCK], relaid[atom_rows - BLOCK :])
    energies, force_ext, new_rows = layer(
        pair_block.reshape(-1),
        rows,
        relaid,
        low,
        high,
        gains,
        radial_weights.reshape(-1, radial_weights.shape[2]),
        mix_weight,
        self_weight,
        readout.reshape(1, -1),
    )
    from_low, from_high = from_sides(force_ext[:3, :BLOCK], force_ext[:3, atom_rows + BLOCK :])
    forces = force_ext[:3, BLOCK : atom_rows + BLOCK]
    forces = forces + jnp.pad(from_low, ((0, 0), (0, atom_rows - BLOCK)))
    forces = forces + jnp.pad(from_high, ((0, 0), (atom_rows - BLOCK, 0)))
    return (energies.reshape(atom_rows), forces.T, new_rows)


def solution(mesh):
    placed = (
        P(("dom", "blk"), None),
        P(("dom", "blk")),
        P(("dom", "blk"), None),
        P(("dom", "blk")),
        P(("dom", "blk")),
        P(("dom", "blk"), None),
        P(),
        P(),
        P(),
        P(),
        P(),
    )
    return jax.shard_map(
        per_device,
        mesh=mesh,
        in_specs=placed,
        out_specs=(P(("dom", "blk")), P(("dom", "blk"), None), P(("dom", "blk"), None)),
        check_vma=False,
    )
```

time: 522 us -> 118 us (0.23)
  the two profiles are of different devices: /device:TPU:4 before, /device:TPU:7 now
where the time goes in v1:
time: 118 us; the launch traced here: 117 us
  Pallas kernels  45.2 us (38%)
  waiting for transfers between devices  31.2 us (26%)
  starting transfers between devices  20.7 us (18%)
  other arithmetic  11.2 us (9%)
  local copies, waits for them, and re-layouts  6.52 us (6%)
  matrix products  1.71 us (1%)
    pallas_call x1, Pallas kernels, layer(): pl.pallas_call(functools.partial(layer_kernel, orders=orders), grid=(tile...  40.7 us
    all_to_all x1, waiting for transfers between devices, per_device(): lax.all_to_all(parcels, AXES, split_axis=0, concat_axis=0, tiled=True)  23.2 us
    ppermute x3, waiting for transfers between devices, from_sides(): high = lax.ppermute(block_low, AXES, backward)  7.92 us
    ppermute x3, starting transfers between devices, from_sides(): low = lax.ppermute(block_high, AXES, forward)  7.32 us
    ppermute x3, starting transfers between devices, from_sides(): high = lax.ppermute(block_low, AXES, backward)  6.94 us
    all_to_all x1, starting transfers between devices, per_device(): lax.all_to_all(parcels, AXES, split_axis=0, concat_axis=0, tiled=True)  6.39 us
    pallas_call x1, Pallas kernels, relay(): pl.pallas_call(relay_kernel, out_shape=jax.ShapeDtypeStruct((rows, cols),...  4.56 us
    gather x2, other arithmetic, per_device(): jnp.repeat(block_count, BLOCK, total_repeat_length=atom_rows)  4.46 us
  transfers between devices with their start and end apart: 7, of which 3 were waited for; matrix products, arithmetic and copies ran while one was open for 13% of the time, Pallas kernels for 4%

profile of v1, /device:TPU:7, one launch (start us, length us, event | category | flops | bytes accessed | tf_op | source)
XLA Modules:
  0.0 117.4 jit_solution(2729232090338898674)
XLA Ops:
  0.7 6.4 %all-to-all-start = ((bf16[32,24,1152]{2,1,0:T(8,128)(2,1)}), bf16[32,24,1152]{2,1,0:T(8,128)(2,1)S(1)}, u32[]{:S(2)}, u32[]{:S(2)}) async-start(bf16[32,24,1152]{2,1,0:T(8,128)(2,1)} %bitcast.67), calls=%async_computation | async-start | bytes 3538944 | tf_op jit(solution)/shard_map/all_to_all | solution.py:363
  7.1 0.1 fusion.17
  7.2 3.3 %collective-permute-start = (f32[3,64]{1,0:T(4,128)S(1)}, f32[3,64]{1,0:T(4,128)S(1)}, u32[]{:S(2)}, u32[]{:S(2)}) collective-permute-start(f32[3,64]{1,0:T(4,128)S(1)} %get-tuple-element.34), channel_id=1, source_target_pairs={{0,1},{1,2},{2,3},{3,4},{4,5},{5,6},{6,7},{7,8},{8,9},{9,10},{10,1... | collective-permute-start | bytes 2312 | tf_op jit(solution)/shard_map/ppermute | solution.py:341
  10.5 1.9 %collective-permute-start.1 = (f32[3,64]{1,0:T(4,128)S(1)}, f32[3,64]{1,0:T(4,128)S(1)}, u32[]{:S(2)}, u32[]{:S(2)}) collective-permute-start(f32[3,64]{1,0:T(4,128)S(1)} %get-tuple-element.35), channel_id=1, source_target_pairs={{1,0},{2,1},{3,2},{4,3},{5,4},{6,5},{7,6},{8,7},{9,8},{10,9},{11,1... | collective-permute-start | bytes 2312 | tf_op jit(solution)/shard_map/ppermute | solution.py:342
  12.5 0.7 fusion.18
  13.2 0.1 fusion.2
  13.3 4.4 %fusion.13 = (s32[768]{0:T(1024)S(1)}, s32[768,1]{0,1:T(1,128)S(1)}) fusion(s32[]{:T(128)} %bitcast.8, s32[]{:T(128)} %bitcast.9, s32[]{:T(128)} %bitcast.10, s32[]{:T(128)} %bitcast.11, s32[]{:T(128)} %bitcast.12, s32[]{:T(128)} %bitcast.14, s32[]{:T(128)} %bitcast.13, s32[1,1,6,128]{3,2,1,0:T(8,128)S(1)} %get-tuple-element.37, ...), kind=kLoop, calls=%fused_computation.35 | loop fusion | flops 10752 | bytes 12316 | tf_op jit(solution)/shard_map/jit(_take)/gather | solution.py:366
  17.7 3.2 %broadcast_select_fusion = (s32[768]{0:T(1024)S(1)}, pred[768]{0:T(1024)(128)(4,1)S(1)}) fusion(s32[768]{0:T(1024)S(1)} %copy-done.7, pred[768]{0:T(1024)(128)(4,1)S(1)} %get-tuple-element.25, pred[768]{0:T(1024)(128)(4,1)S(1)} %get-tuple-element.24, pred[768]{0:T(1024)(128)(4,1)S(1)} %get-tuple-element.23, pred[768]{0:T(1024)(128)(4,1)S(1)} %get-tuple-element.22, ...), kind=kLoop, calls=%fused_computation.36 | loop fusion | flops 16896 | bytes 16940 | tf_op jit(solution)/shard_map/jit(_where)/select_n | solution.py:367
  20.9 0.6 reshape.120.arrival_ref
  21.5 0.1 pad_convert_fusion
  21.6 0.1 copy.17
  21.8 0.6 reshape.124.radial_ref
  22.4 0.1 copy.16
  22.5 0.6 reshape.117.pair_ref
  23.1 0.1 pad.23.clone
  23.1 1.7 %fusion.gains_ref = f32[768,384]{1,0:T(8,128)} fusion(f32[89,384]{1,0:T(8,128)S(1)} %bitcast.70, s32[768]{0:T(1024)S(1)} %copy-done.6), kind=kOutput, calls=%fused_computation.1 | convolution fusion | flops 315034368 | bytes 1319424 | tf_op jit(solution)/shard_map/dot_general | solution.py:377
  24.8 23.2 %all-to-all-done = bf16[32,24,1152]{2,1,0:T(8,128)(2,1)S(1)} async-done(((bf16[32,24,1152]{2,1,0:T(8,128)(2,1)}), bf16[32,24,1152]{2,1,0:T(8,128)(2,1)S(1)}, u32[]{:S(2)}, u32[]{:S(2)}) %all-to-all-start) | async-done | bytes 1769504 | tf_op jit(solution)/shard_map/all_to_all | solution.py:363
  48.1 1.2 %copy-done = bf16[32,24,1152]{2,1,0:T(8,128)(2,1)} copy-done((bf16[32,24,1152]{2,1,0:T(8,128)(2,1)}, bf16[32,24,1152]{2,1,0:T(8,128)(2,1)S(1)}, u32[]{:S(2)}) %copy-start) | copy-done | bytes 1769496
  49.3 4.6 %relay.1.relaid_ref = bf16[768,1152]{1,0:T(8,128)(2,1)} custom-call(s32[1,768]{1,0:T(1,128)} %reshape.120.arrival_ref, bf16[768,1152]{1,0:T(8,128)(2,1)} %bitcast.68), custom_call_target="tpu_custom_call" | custom-call | flops 1358954496 | bytes 3538944 | tf_op jit(solution)/shard_map/relay/pallas_call | solution.py:39
  53.9 1.0 fusion.15
  54.9 2.1 %collective-permute-start.2 = (bf16[64,1152]{1,0:T(8,128)(2,1)S(1)}, bf16[64,1152]{1,0:T(8,128)(2,1)S(1)}, u32[]{:S(2)}, u32[]{:S(2)}) collective-permute-start(bf16[64,1152]{1,0:T(8,128)(2,1)S(1)} %get-tuple-element.31), channel_id=1, source_target_pairs={{0,1},{1,2},{2,3},{3,4},{4,5},{5,6},{6,7},{7,8},{8,9},{9,10},{10,1... | collective-permute-start | bytes 442376 | tf_op jit(solution)/shard_map/ppermute | solution.py:341
  57.0 2.6 %collective-permute-start.3 = (bf16[64,1152]{1,0:T(8,128)(2,1)S(1)}, bf16[64,1152]{1,0:T(8,128)(2,1)S(1)}, u32[]{:S(2)}, u32[]{:S(2)}) collective-permute-start(bf16[64,1152]{1,0:T(8,128)(2,1)S(1)} %get-tuple-element.30), channel_id=1, source_target_pairs={{1,0},{2,1},{3,2},{4,3},{5,4},{6,5},{7,6},{8,7},{9,8},{10,9},{11,1... | collective-permute-start | bytes 442376 | tf_op jit(solution)/shard_map/ppermute | solution.py:342
  59.6 0.7 maximum_maximum_fusion.rows_ref
  60.3 4.9 %collective-permute-done.3.high_ref = bf16[64,1152]{1,0:T(8,128)(2,1)S(1)} collective-permute-done((bf16[64,1152]{1,0:T(8,128)(2,1)S(1)}, bf16[64,1152]{1,0:T(8,128)(2,1)S(1)}, u32[]{:S(2)}, u32[]{:S(2)}) %collective-permute-start.3) | collective-permute-done | bytes 147488 | tf_op jit(solution)/shard_map/ppermute | solution.py:342
  65.2 0.7 copy-done.10
  65.9 40.7 %layer.1 = (f32[6,1,128]{2,1,0:T(1,128)}, f32[8,896]{1,0:T(8,128)}, bf16[768,128]{1,0:T(8,128)(2,1)}) custom-call(s32[36]{0:T(128)} %reshape.117.pair_ref, f32[8,896]{1,0:T(8,128)} %maximum_maximum_fusion.rows_ref, bf16[768,1152]{1,0:T(8,128)(2,1)} %relay.1.relaid_ref, bf16[64,1152]{1,0:T(8,128)(2,1)} %copy-done.9, bf16[64,1152]{1,0:T(8,128)(2,1)} %copy-done.10, ...), custom_call_target="tpu_custom_call" | custom-call | flops 20132659200 | bytes 3538944 | tf_op jit(solution)/shard_map/layer/pallas_call | solution.py:304
  106.6 0.8 fusion.16
  107.3 1.9 %collective-permute-start.4 = (f32[3,64]{1,0:T(4,128)S(1)}, f32[3,64]{1,0:T(4,128)S(1)}, u32[]{:S(2)}, u32[]{:S(2)}) collective-permute-start(f32[3,64]{1,0:T(4,128)S(1)} %get-tuple-element.32), channel_id=1, source_target_pairs={{0,1},{1,2},{2,3},{3,4},{4,5},{5,6},{6,7},{7,8},{8,9},{9,10},{10,1... | collective-permute-start | bytes 2312 | tf_op jit(solution)/shard_map/ppermute | solution.py:341
  109.2 2.4 %collective-permute-start.5 = (f32[3,64]{1,0:T(4,128)S(1)}, f32[3,64]{1,0:T(4,128)S(1)}, u32[]{:S(2)}, u32[]{:S(2)}) collective-permute-start(f32[3,64]{1,0:T(4,128)S(1)} %get-tuple-element.33), channel_id=1, source_target_pairs={{1,0},{2,1},{3,2},{4,3},{5,4},{6,5},{7,6},{8,7},{9,8},{10,9},{11,1... | collective-permute-start | bytes 2312 | tf_op jit(solution)/shard_map/ppermute | solution.py:342
  111.7 1.3 %reduce.8 = f32[6,128]{1,0:T(8,128)} reduce(f32[6,1,128]{2,1,0:T(1,128)} %get-tuple-element.18, f32[]{:T(128)} %constant.134), dimensions={1}, to_apply=%get-tuple-element.18.reduce_sub_computation | reduce | bytes 6148 | tf_op jit(solution)/shard_map/layer/pallas_call | solution.py:304
  112.9 3.0 %collective-permute-done.5 = f32[3,64]{1,0:T(4,128)S(1)} collective-permute-done((f32[3,64]{1,0:T(4,128)S(1)}, f32[3,64]{1,0:T(4,128)S(1)}, u32[]{:S(2)}, u32[]{:S(2)}) %collective-permute-start.5) | collective-permute-done | bytes 800 | tf_op jit(solution)/shard_map/ppermute | solution.py:342
  115.9 1.4 %add_bitcast_fusion = f32[768,3]{0,1:T(4,128)} fusion(f32[3,64]{1,0:T(4,128)S(1)} %collective-permute-done.5, f32[3,64]{1,0:T(4,128)S(1)} %collective-permute-done.4, f32[8,896]{1,0:T(8,128)} %get-tuple-element.19), kind=kLoop, calls=%fused_computation.5 | loop fusion | flops 4608 | bytes 19968 | tf_op jit(solution)/shard_map/transpose | solution.py:398
  (31 shorter events, 0.2 us)
Async XLA Ops:
  0.6 6.5 %copy-start.4 = (f32[768,3]{0,1:T(4,128)S(1)}, f32[768,3]{0,1:T(4,128)}, u32[]{:S(2)}) copy-start(f32[768,3]{0,1:T(4,128)} %param.15) | copy-start | bytes 27652
  0.6 11.8 %copy-start.2 = (s32[12]{0:T(128)S(1)}, s32[12]{0:T(128)}, u32[]{:S(2)}) copy-start(s32[12]{0:T(128)} %param.17) | copy-start | bytes 148
  0.7 12.5 %copy-start.5 = (s32[6,128]{1,0:T(8,128)S(1)}, s32[6,128]{1,0:T(8,128)}, u32[]{:S(2)}) copy-start(s32[6,128]{1,0:T(8,128)} %constant.102.clone.1) | copy-start | bytes 9220
  0.7 17.1 %copy-start.7 = (s32[768]{0:T(1024)S(1)}, s32[768]{0:T(1024)}, u32[]{:S(2)}) copy-start(s32[768]{0:T(1024)} %param.14) | copy-start | bytes 9220
  0.7 20.9 %copy-start.1 = (f32[89,3,128]{2,0,1:T(8,128)S(1)}, f32[89,3,128]{2,0,1:T(8,128)}, u32[]{:S(2)}) copy-start(f32[89,3,128]{2,0,1:T(8,128)} %param.20) | copy-start | bytes 410116
  0.7 21.1 %copy-start.3 = (f32[8,7,128]{2,0,1:T(8,128)S(1)}, f32[8,7,128]{2,0,1:T(8,128)}, u32[]{:S(2)}) copy-start(f32[8,7,128]{2,0,1:T(8,128)} %param.19) | copy-start | bytes 86020
  0.7 21.7 %copy-start.8 = (s32[12,3]{0,1:T(4,128)S(1)}, s32[12,3]{0,1:T(4,128)}, u32[]{:S(2)}) copy-start(s32[12,3]{0,1:T(4,128)} %param.18) | copy-start | bytes 436
  0.7 22.4 %copy-start.6 = (s32[768]{0:T(1024)S(1)}, s32[768]{0:T(1024)}, u32[]{:S(2)}) copy-start(s32[768]{0:T(1024)} %param.16) | copy-start | bytes 9220
  0.7 47.4 %all-to-all-start = ((bf16[32,24,1152]{2,1,0:T(8,128)(2,1)}), bf16[32,24,1152]{2,1,0:T(8,128)(2,1)S(1)}, u32[]{:S(2)}, u32[]{:S(2)}) async-start(bf16[32,24,1152]{2,1,0:T(8,128)(2,1)} %bitcast.67), calls=%async_computation | async-start | bytes 3538944 | tf_op jit(solution)/shard_map/all_to_all | solution.py:363
  7.2 52.4 %collective-permute-start = (f32[3,64]{1,0:T(4,128)S(1)}, f32[3,64]{1,0:T(4,128)S(1)}, u32[]{:S(2)}, u32[]{:S(2)}) collective-permute-start(f32[3,64]{1,0:T(4,128)S(1)} %get-tuple-element.34), channel_id=1, source_target_pairs={{0,1},{1,2},{2,3},{3,4},{4,5},{5,6},{6,7},{7,8},{8,9},{9,10},{10,1... | collective-permute-start | bytes 2312 | tf_op jit(solution)/shard_map/ppermute | solution.py:341
  10.5 49.1 %collective-permute-start.1 = (f32[3,64]{1,0:T(4,128)S(1)}, f32[3,64]{1,0:T(4,128)S(1)}, u32[]{:S(2)}, u32[]{:S(2)}) collective-permute-start(f32[3,64]{1,0:T(4,128)S(1)} %get-tuple-element.35), channel_id=1, source_target_pairs={{1,0},{2,1},{3,2},{4,3},{5,4},{6,5},{7,6},{8,7},{9,8},{10,9},{11,1... | collective-permute-start | bytes 2312 | tf_op jit(solution)/shard_map/ppermute | solution.py:342
  48.1 1.2 %copy-start = (bf16[32,24,1152]{2,1,0:T(8,128)(2,1)}, bf16[32,24,1152]{2,1,0:T(8,128)(2,1)S(1)}, u32[]{:S(2)}) copy-start(bf16[32,24,1152]{2,1,0:T(8,128)(2,1)S(1)} %all-to-all-done) | copy-start | bytes 5308420
  54.9 5.4 %collective-permute-start.2 = (bf16[64,1152]{1,0:T(8,128)(2,1)S(1)}, bf16[64,1152]{1,0:T(8,128)(2,1)S(1)}, u32[]{:S(2)}, u32[]{:S(2)}) collective-permute-start(bf16[64,1152]{1,0:T(8,128)(2,1)S(1)} %get-tuple-element.31), channel_id=1, source_target_pairs={{0,1},{1,2},{2,3},{3,4},{4,5},{5,6},{6,7},{7,8},{8,9},{9,10},{10,1... | collective-permute-start | bytes 442376 | tf_op jit(solution)/shard_map/ppermute | solution.py:341
  57.0 8.3 %collective-permute-start.3 = (bf16[64,1152]{1,0:T(8,128)(2,1)S(1)}, bf16[64,1152]{1,0:T(8,128)(2,1)S(1)}, u32[]{:S(2)}, u32[]{:S(2)}) collective-permute-start(bf16[64,1152]{1,0:T(8,128)(2,1)S(1)} %get-tuple-element.30), channel_id=1, source_target_pairs={{1,0},{2,1},{3,2},{4,3},{5,4},{6,5},{7,6},{8,7},{9,8},{10,9},{11,1... | collective-permute-start | bytes 442376 | tf_op jit(solution)/shard_map/ppermute | solution.py:342
  60.3 4.9 %copy-start.9 = (bf16[64,1152]{1,0:T(8,128)(2,1)}, bf16[64,1152]{1,0:T(8,128)(2,1)S(1)}, u32[]{:S(2)}) copy-start(bf16[64,1152]{1,0:T(8,128)(2,1)S(1)} %collective-permute-done.2.low_ref) | copy-start | bytes 442372
  65.2 0.7 copy-start.10
  107.3 5.6 %collective-permute-start.4 = (f32[3,64]{1,0:T(4,128)S(1)}, f32[3,64]{1,0:T(4,128)S(1)}, u32[]{:S(2)}, u32[]{:S(2)}) collective-permute-start(f32[3,64]{1,0:T(4,128)S(1)} %get-tuple-element.32), channel_id=1, source_target_pairs={{0,1},{1,2},{2,3},{3,4},{4,5},{5,6},{6,7},{7,8},{8,9},{9,10},{10,1... | collective-permute-start | bytes 2312 | tf_op jit(solution)/shard_map/ppermute | solution.py:341
  109.2 6.7 %collective-permute-start.5 = (f32[3,64]{1,0:T(4,128)S(1)}, f32[3,64]{1,0:T(4,128)S(1)}, u32[]{:S(2)}, u32[]{:S(2)}) collective-permute-start(f32[3,64]{1,0:T(4,128)S(1)} %get-tuple-element.33), channel_id=1, source_target_pairs={{1,0},{2,1},{3,2},{4,3},{5,4},{6,5},{7,6},{8,7},{9,8},{10,9},{11,1... | collective-permute-start | bytes 2312 | tf_op jit(solution)/shard_map/ppermute | solution.py:342

commit v2 on v0

v2 whole, which is shorter than its diff:
```python
import functools
import math

import jax
import jax.numpy as jnp
import numpy as np
from jax import lax
from jax.experimental import pallas as pl
from jax.experimental.pallas import tpu as pltpu
from jax.sharding import PartitionSpec as P

BLOCK = 64
TILE = 2 * BLOCK
WINDOW = 4 * BLOCK
SUB = 32
HARM = 9
PATHS = 7
ROOT_THREE = math.sqrt(3.0)
AXES = ("dom", "blk")
VMEM_BYTES = 48 * 1024 * 1024
HELD = pltpu.VMEM


def degree(k):
    return 0 if k == 0 else (1 if k < 4 else 2)


def polynomial(square, coefficients):
    total = jnp.full_like(square, coefficients[-1])
    for value in coefficients[-2::-1]:
        total = total * square + value
    return total


SINE = [(-1.0) ** m * math.pi ** (2 * m + 1) / math.factorial(2 * m + 1) for m in range(6)]
COSINE = [(-1.0) ** m * math.pi ** (2 * m) / math.factorial(2 * m) for m in range(7)]


def solid(x, y, z):
    return [
        None,
        x,
        y,
        z,
        ROOT_THREE * x * y,
        ROOT_THREE * y * z,
        z * z - 0.5 * (x * x + y * y),
        ROOT_THREE * z * x,
        (0.5 * ROOT_THREE) * (x * x - y * y),
    ]


def chosen_rows(wanted, rows):
    source = lax.broadcasted_iota(jnp.int32, (wanted.shape[0], rows), 1)
    return (wanted == source).astype(jnp.float32).astype(jnp.bfloat16)


def as_column(row_ref):
    return jnp.transpose(jnp.broadcast_to(row_ref[...], (8, row_ref.shape[1])))[:, 0:1]


def edge_tiles_kernel(arrival_ref, received_ref, first_ref, last_ref):
    rows = received_ref.shape[0]
    wanted = as_column(arrival_ref)
    both = jnp.concatenate([wanted[0:TILE], wanted[rows - TILE :]], axis=0)
    found = jnp.dot(
        chosen_rows(both, rows), received_ref[...], preferred_element_type=jnp.float32
    ).astype(jnp.bfloat16)
    first_ref[...] = found[0:TILE]
    last_ref[...] = found[TILE:]


def pair_factors(base, rows_ref, cols_ref, edge_at, value_at, change_at, orders):
    window = pl.ds(base, WINDOW)
    for sub in range(TILE // SUB):
        half = sub * SUB // BLOCK
        here = pl.ds(pl.multiple_of(base + (BLOCK + sub * SUB), SUB), SUB)
        column = lax.broadcasted_iota(jnp.int32, (SUB, WINDOW), 1)
        row = lax.broadcasted_iota(jnp.int32, (SUB, WINDOW), 0) + (sub * SUB + BLOCK)
        offset = column - half * BLOCK
        low = jnp.where((offset >= 0) & (offset < BLOCK), cols_ref[here, 5:6], 0.0)
        high = jnp.where(
            (offset >= 2 * BLOCK) & (offset < 3 * BLOCK), cols_ref[here, 6:7], low
        )
        same = (offset >= BLOCK) & (offset < 2 * BLOCK) & (row != column)
        keep = jnp.where(same, 1.0, high)
        x, y, z = [rows_ref[a : a + 1, window] - cols_ref[here, a : a + 1] for a in range(3)]
        spread = x * x + y * y + z * z
        room = jnp.maximum(1.0 - spread, 0.0)
        squared = room * room * keep
        envelope = squared * room
        slope = -3.0 * squared
        shifted = jnp.minimum(spread, 1.0) - 0.5
        shifted_sq = shifted * shifted
        cosine = -shifted * polynomial(shifted_sq, SINE)
        sine = polynomial(shifted_sq, COSINE)
        twice = 2.0 * cosine
        cos_prev, cos_now = jnp.ones_like(cosine), cosine
        sin_prev, sin_now = jnp.zeros_like(sine), sine
        harm = solid(x, y, z)
        for n in range(orders):
            rows = slice(n * SUB, (n + 1) * SUB)
            if n == 0:
                value, change = envelope, slope
            else:
                value = envelope * cos_now
                change = slope * cos_now - (n * math.pi) * (envelope * sin_now)
            value_at[sub, rows, :] = value
            change_at[sub, rows, :] = change
            for k in range(HARM):
                edge = value if k == 0 else value * harm[k]
                edge_at[sub, k, rows, :] = edge.astype(jnp.bfloat16)
            if n >= 1:
                cos_prev, cos_now = cos_now, twice * cos_now - cos_prev
                sin_prev, sin_now = sin_now, twice * sin_now - sin_prev


def pairs_kernel(rows_ref, edge_ref, value_ref, change_ref, cols_ref, orders):
    tile = pl.program_id(0)

    @pl.when(tile == 0)
    def _():
        cols_ref[...] = jnp.transpose(rows_ref[...])

    base = pl.multiple_of(tile * TILE, TILE)
    pair_factors(
        base, rows_ref, cols_ref, edge_ref.at[0], value_ref.at[0], change_ref.at[0], orders
    )


def spread_weights(radial_ref, narrow_ref, orders):
    for path in range(PATHS):
        for n in range(orders):
            row = radial_ref[n * PATHS + path : n * PATHS + path + 1, :]
            narrow_ref[path, n * SUB : (n + 1) * SUB, :] = jnp.broadcast_to(
                row, (SUB, row.shape[1])
            ).astype(jnp.bfloat16)


def fetch(sources, held):
    edge_hbm, value_hbm, change_hbm = sources
    edge_ref, value_ref, change_ref, edge_sem, factor_sem = held
    count, subs = edge_ref.shape[:2]

    def edges(at, sub):
        return pltpu.make_async_copy(
            edge_hbm.at[at, sub], edge_ref.at[at, sub], edge_sem.at[at, sub]
        )

    def factors(at):
        return (
            pltpu.make_async_copy(value_hbm.at[at], value_ref.at[at], factor_sem.at[at, 0]),
            pltpu.make_async_copy(change_hbm.at[at], change_ref.at[at], factor_sem.at[at, 1]),
        )

    for at in range(count):
        for sub in range(subs):
            edges(at, sub).start()
        for copy in factors(at):
            copy.start()
    return edges, factors


def one_tile(at, base, refs, gain_of, copies, results, orders):
    feat_ref, turned_ref, rows_ref, cols_ref, edge_ref, value_ref, change_ref = refs[:7]
    radial_ref, narrow_ref, mix_ref, self_ref, readout_ref = refs[7:12]
    message_ref, grad_ref = refs[12:]
    channels = mix_ref.shape[0]
    window = pl.ds(base, WINDOW)
    centre = pl.ds(pl.multiple_of(base + BLOCK, BLOCK), TILE)
    subs = range(TILE // SUB)

    def weight(n, path):
        return radial_ref[n * PATHS + path : n * PATHS + path + 1, :]

    def piece(k):
        return feat_ref[window, k * channels : (k + 1) * channels]

    def path_sum(product, first, path):
        total = None
        for n in range(orders):
            part = product[n * SUB : (n + 1) * SUB, first : first + channels] * weight(n, path)
            total = part if total is None else total + part
        return total

    for sub in subs:
        rows = slice(sub * SUB, (sub + 1) * SUB)
        if copies is not None:
            copies[0](at, sub).wait()
        for k in range(0, HARM, 2):
            last = min(k + 2, HARM)
            pairs = jnp.dot(
                edge_ref[at, sub, 0],
                feat_ref[window, k * channels : last * channels],
                preferred_element_type=jnp.float32,
            )
            for which in range(k, last):
                path = 0 if which == 0 else 2 + degree(which)
                message_ref[which, rows, :] = path_sum(pairs, (which - k) * channels, path)
        for k in range(1, HARM):
            both = jnp.concatenate([piece(k), piece(0)], axis=1)
            pairs = jnp.dot(edge_ref[at, sub, k], both, preferred_element_type=jnp.float32)
            message_ref[0, rows, :] += path_sum(pairs, 0, 4 + degree(k))
            message_ref[k, rows, :] += path_sum(pairs, channels, degree(k))

    gain = gain_of(centre)
    zero = message_ref[0]
    first = sum(message_ref[k] * message_ref[k] for k in range(1, 4))
    second = sum(message_ref[k] * message_ref[k] for k in range(4, HARM))
    basis = zero + gain[0] * (zero * zero) + gain[1] * first + gain[2] * second
    live = cols_ref[centre, 3:4]
    mixed = jnp.dot(
        basis.astype(jnp.bfloat16), mix_ref[...], preferred_element_type=jnp.float32
    ) + jnp.dot(feat_ref[centre, 0:channels], self_ref[...], preferred_element_type=jnp.float32)
    gate = 1.0 / (1.0 + jnp.exp(-mixed))
    silu = mixed * gate
    readout = readout_ref[...]
    fresh = (live * mixed).astype(jnp.bfloat16)
    energy = jnp.sum(jnp.transpose(live * (readout * silu)), axis=0, keepdims=True)
    mixed_grad = live * readout * (gate * (1.0 + mixed - silu))
    basis_grad = lax.dot_general(
        mixed_grad.astype(jnp.bfloat16),
        mix_ref[...],
        (((1,), (1,)), ((), ())),
        preferred_element_type=jnp.float32,
    )
    grad_ref[0] = (basis_grad * (1.0 + 2.0 * gain[0] * zero)).astype(jnp.bfloat16)
    for k in range(1, HARM):
        grad_ref[k] = (basis_grad * (2.0 * gain[degree(k)]) * message_ref[k]).astype(jnp.bfloat16)

    def backward(sub):
        rows = slice(sub * SUB, (sub + 1) * SUB)
        here = pl.ds(pl.multiple_of(base + (BLOCK + sub * SUB), SUB), SUB)
        grads = [jnp.concatenate([grad_ref[k, rows, :]] * orders, axis=0) for k in range(HARM)]
        x, y, z = [rows_ref[a : a + 1, window] - cols_ref[here, a : a + 1] for a in range(3)]
        harm = solid(x, y, z)
        root_x, root_y, root_z = ROOT_THREE * x, ROOT_THREE * y, ROOT_THREE * z
        slopes = {
            1: {0: None},
            2: {1: None},
            3: {2: None},
            4: {0: root_y, 1: root_x},
            5: {1: root_z, 2: root_y},
            6: {0: -x, 1: -y, 2: 2.0 * z},
            7: {0: root_z, 2: root_x},
            8: {0: root_x, 1: -root_y},
        }

        def over_orders(cross, factor_ref):
            total = None
            for n in range(orders):
                part = cross[n * SUB : (n + 1) * SUB] * factor_ref[
                    at, sub, n * SUB : (n + 1) * SUB, :
                ]
                total = part if total is None else total + part
            return total

        left = jnp.concatenate(
            [grads[k] * narrow_ref[0 if k == 0 else 2 + degree(k)] for k in range(HARM)], axis=1
        )
        cross = jnp.dot(left, turned_ref[:, window], preferred_element_type=jnp.float32)
        radial_total = over_orders(cross, change_ref)
        pull = [None, None, None]
        for k in range(1, HARM):
            left = jnp.concatenate(
                [grads[0] * narrow_ref[4 + degree(k)], grads[k] * narrow_ref[degree(k)]], axis=1
            )
            both = jnp.concatenate(
                [
                    turned_ref[k * channels : (k + 1) * channels, window],
                    turned_ref[0:channels, window],
                ],
                axis=0,
            )
            cross = jnp.dot(left, both, preferred_element_type=jnp.float32)
            along = over_orders(cross, value_ref)
            radial_total = radial_total + over_orders(cross, change_ref) * harm[k]
            for axis, factor in slopes[k].items():
                term = along if factor is None else along * factor
                pull[axis] = term if pull[axis] is None else pull[axis] + term
        radial_total = 2.0 * radial_total
        return [pull[axis] + delta * radial_total for axis, delta in enumerate((x, y, z))]

    if copies is not None:
        for copy in copies[1](at):
            copy.wait()
    onto_window = [None, None, None]
    columns_out = [[], [], []]
    for sub in subs:
        for axis, total in enumerate(backward(sub)):
            summed = jnp.sum(total, axis=0, keepdims=True)
            onto_window[axis] = summed if sub == 0 else onto_window[axis] + summed
            columns_out[axis].append(jnp.sum(total, axis=1, keepdims=True))
    lane = lax.broadcasted_iota(jnp.int32, (TILE, 8), 1)
    row = lax.broadcasted_iota(jnp.int32, (8, WINDOW), 0)
    packed = jnp.zeros((TILE, 8), jnp.float32)
    pulled = jnp.zeros((8, WINDOW), jnp.float32)
    for axis in range(3):
        packed = jnp.where(lane == axis, jnp.concatenate(columns_out[axis], axis=0), packed)
        pulled = jnp.where(row == axis, onto_window[axis], pulled)
    turned = jnp.transpose(packed)
    side = jnp.zeros((8, BLOCK), jnp.float32)
    results(fresh, energy, jnp.concatenate([side, turned, side], axis=1) - pulled)


def inner_kernel(
    arrival_ref,
    received_ref,
    rows_ref,
    edge_hbm,
    value_hbm,
    change_hbm,
    gains_ref,
    radial_ref,
    mix_ref,
    self_ref,
    readout_ref,
    feat_ref,
    new_ref,
    energy_ref,
    force_ref,
    turned_ref,
    cols_ref,
    narrow_ref,
    message_ref,
    grad_ref,
    edge_ref,
    value_ref,
    change_ref,
    edge_sem,
    factor_sem,
    orders,
):
    held = (edge_ref, value_ref, change_ref, edge_sem, factor_sem)
    copies = fetch((edge_hbm, value_hbm, change_hbm), held)
    rows = received_ref.shape[0]
    channels = mix_ref.shape[0]
    wanted = as_column(arrival_ref)
    cols_ref[...] = jnp.transpose(rows_ref[...])
    spread_weights(radial_ref, narrow_ref, orders)
    force_ref[...] = jnp.zeros_like(force_ref)
    for part in range(rows // TILE):
        here = slice(part * TILE, (part + 1) * TILE)
        found = jnp.dot(
            chosen_rows(wanted[here], rows),
            received_ref[...],
            preferred_element_type=jnp.float32,
        ).astype(jnp.bfloat16)
        feat_ref[here, :] = found
        turned_ref[:, here] = jnp.transpose(found)
    refs = (feat_ref, turned_ref, rows_ref, cols_ref, edge_ref, value_ref, change_ref)
    refs += (radial_ref, narrow_ref, mix_ref, self_ref, readout_ref, message_ref, grad_ref)

    def gain_of(centre):
        return [gains_ref[centre, l * channels : (l + 1) * channels] for l in range(3)]

    def body(at, carry):
        base = pl.multiple_of(at * TILE, TILE)

        def results(fresh, energy, force):
            new_ref[at] = fresh
            energy_ref[at] = energy
            force_ref[:, pl.ds(base, WINDOW)] += force

        one_tile(at, base, refs, gain_of, copies, results, orders)
        return carry

    lax.fori_loop(0, edge_hbm.shape[0], body, 0)


def outer_kernel(
    low_ref,
    high_ref,
    feat_ref,
    low_rows_ref,
    rows_ref,
    high_rows_ref,
    table_ref,
    radial_ref,
    mix_ref,
    self_ref,
    readout_ref,
    inner_new_ref,
    inner_energy_ref,
    inner_force_ref,
    new_ref,
    energy_ref,
    force_ref,
    near_ref,
    turned_ref,
    near_rows_ref,
    cols_ref,
    narrow_ref,
    message_ref,
    grad_ref,
    edge_ref,
    value_ref,
    change_ref,
    total_ref,
    orders,
):
    rows = feat_ref.shape[0]
    channels = mix_ref.shape[0]
    near_rows_ref[:, 0:TILE] = low_rows_ref[...]
    near_rows_ref[:, TILE : 2 * TILE] = rows_ref[:, 0:TILE]
    near_rows_ref[:, 2 * TILE : 3 * TILE] = rows_ref[:, rows - TILE :]
    near_rows_ref[:, 3 * TILE :] = high_rows_ref[...]
    cols_ref[...] = jnp.transpose(near_rows_ref[...])
    spread_weights(radial_ref, narrow_ref, orders)
    near_ref[0:TILE, :] = low_ref[...]
    near_ref[TILE : 2 * TILE, :] = feat_ref[0:TILE, :]
    near_ref[2 * TILE : 3 * TILE, :] = feat_ref[rows - TILE :, :]
    near_ref[3 * TILE :, :] = high_ref[...]
    for part in range(4):
        here = slice(part * TILE, (part + 1) * TILE)
        turned_ref[:, here] = jnp.transpose(near_ref[here, :])
    refs = (near_ref, turned_ref, near_rows_ref, cols_ref, edge_ref, value_ref, change_ref)
    refs += (radial_ref, narrow_ref, mix_ref, self_ref, readout_ref, message_ref, grad_ref)

    def gain_of(centre):
        kinds = lax.broadcasted_iota(jnp.int32, (TILE, table_ref.shape[0]), 1)
        picked = (cols_ref[centre, 4:5].astype(jnp.int32) == kinds).astype(jnp.float32)
        rows_of = jnp.dot(
            picked,
            table_ref[...],
            precision=lax.Precision.HIGHEST,
            preferred_element_type=jnp.float32,
        )
        return [rows_of[:, l * channels : (l + 1) * channels] for l in range(3)]

    def body(at, carry):
        base = pl.multiple_of(at * WINDOW, WINDOW)

        def results(fresh, energy, force):
            total_ref[at] = force

            @pl.when(at == 0)
            def _():
                new_ref[0:BLOCK, :] = fresh[BLOCK:, :]
                energy_ref[:, 0:BLOCK] = energy[:, BLOCK:]

            @pl.when(at == 1)
            def _():
                new_ref[rows - BLOCK :, :] = fresh[0:BLOCK, :]
                energy_ref[:, rows - BLOCK :] = energy[:, 0:BLOCK]

        pair_factors(
            base, near_rows_ref, cols_ref, edge_ref.at[at], value_ref.at[at], change_ref.at[at], orders
        )
        one_tile(at, base, refs, gain_of, None, results, orders)
        return carry

    lax.fori_loop(0, 2, body, 0)
    inner = inner_new_ref.shape[0]
    for at in range(inner):
        here = slice(BLOCK + at * TILE, BLOCK + (at + 1) * TILE)
        new_ref[here, :] = inner_new_ref[at]
        energy_ref[:, here] = inner_energy_ref[at]
    force_ref[...] = inner_force_ref[...]
    force_ref[:, 0:TILE] += total_ref[0, :, TILE:]
    force_ref[:, rows - TILE :] += total_ref[1, :, 0:TILE]


def call(kernel, name, out_shape, scratch, flops, *operands, distant=()):
    whole = pl.BlockSpec(memory_space=pltpu.VMEM)
    hbm = pl.BlockSpec(memory_space=pl.ANY)
    return pl.pallas_call(
        kernel,
        out_shape=out_shape,
        in_specs=[hbm if at in distant else whole for at in range(len(operands))],
        out_specs=jax.tree.map(lambda _: whole, out_shape),
        scratch_shapes=scratch,
        compiler_params=pltpu.CompilerParams(vmem_limit_bytes=VMEM_BYTES),
        cost_estimate=pl.CostEstimate(flops=flops, bytes_accessed=4 * 2**20, transcendentals=0),
        name=name,
    )(*operands)


def from_sides(block_low, block_high):
    count = lax.axis_size(AXES)
    forward = [(i, i + 1) for i in range(count - 1)]
    backward = [(target, source) for source, target in forward]
    low = lax.ppermute(block_high, AXES, forward)
    high = lax.ppermute(block_low, AXES, backward)
    return low, high


def per_device(
    features_domain,
    arrival,
    positions,
    species,
    block_count,
    pair_block,
    radial_weights,
    species_weights,
    mix_weight,
    self_weight,
    readout,
):
    devices = lax.axis_size(AXES)
    atom_rows, feature_cols = features_domain.shape
    piece_rows = atom_rows // devices
    parcels = features_domain.reshape(devices, piece_rows, feature_cols)
    received = lax.all_to_all(parcels, AXES, split_axis=0, concat_axis=0, tiled=True)
    received = received.reshape(atom_rows, feature_cols)
    blocks = block_count.shape[0]
    bf16, f32 = jnp.bfloat16, jnp.float32
    shape = jax.ShapeDtypeStruct

    def per_slot(values):
        return jnp.broadcast_to(values[:, None], (blocks, BLOCK)).reshape(1, atom_rows)

    slot = jnp.arange(BLOCK, dtype=jnp.int32)
    live = (slot[None, :] < block_count[:, None]).reshape(1, atom_rows)
    arrival_live = jnp.where(live, arrival.reshape(1, atom_rows), -1)
    listed = (pair_block >= 0).astype(f32)
    rows = jnp.concatenate(
        [
            positions.T,
            live.astype(f32),
            species.astype(f32).reshape(1, atom_rows),
            per_slot(listed[:, 0]),
            per_slot(listed[:, 2]),
            jnp.zeros((1, atom_rows), f32),
        ],
        axis=0,
    )
    low_rows, high_rows = from_sides(rows[:, :TILE], rows[:, atom_rows - TILE :])
    species_total = species_weights.shape[0]
    one_hot = (species[:, None] == jnp.arange(species_total, dtype=jnp.int32)[None, :]).astype(f32)
    table = species_weights.reshape(species_total, -1)
    gains = jnp.dot(one_hot, table, precision=lax.Precision.HIGHEST)
    orders, _, channels = radial_weights.shape
    inner = atom_rows // TILE - 1
    subs = TILE // SUB
    stack = orders * SUB
    edges, values, changes = pl.pallas_call(
        functools.partial(pairs_kernel, orders=orders),
        grid=(inner,),
        out_shape=(
            pltpu.HBM((inner, subs, HARM, stack, WINDOW), bf16),
            pltpu.HBM((inner, subs, stack, WINDOW), f32),
            pltpu.HBM((inner, subs, stack, WINDOW), f32),
        ),
        in_specs=[pl.BlockSpec((8, atom_rows), lambda t: (0, 0))],
        out_specs=(
            pl.BlockSpec((1, subs, HARM, stack, WINDOW), lambda t: (t, 0, 0, 0, 0)),
            pl.BlockSpec((1, subs, stack, WINDOW), lambda t: (t, 0, 0, 0)),
            pl.BlockSpec((1, subs, stack, WINDOW), lambda t: (t, 0, 0, 0)),
        ),
        scratch_shapes=[pltpu.VMEM((atom_rows, 8), f32)],
        compiler_params=pltpu.CompilerParams(vmem_limit_bytes=VMEM_BYTES),
        cost_estimate=pl.CostEstimate(flops=10**10, bytes_accessed=40 * 2**20, transcendentals=0),
        name="pairs",
    )(rows)
    first, last = call(
        edge_tiles_kernel,
        "edge_tiles",
        (shape((TILE, feature_cols), bf16), shape((TILE, feature_cols), bf16)),
        [],
        4 * TILE * atom_rows * feature_cols,
        arrival_live,
        received,
    )
    low, high = from_sides(first, last)
    radial = radial_weights.reshape(-1, channels)
    common = (radial, mix_weight, self_weight, readout.reshape(1, -1))
    tile_flops = 4 * orders * TILE * WINDOW * channels * 25
    held = functools.partial(pltpu.with_memory_space_constraint, memory_space=pltpu.VMEM)
    distant = functools.partial(pltpu.with_memory_space_constraint, memory_space=pltpu.HBM)

    def scratch(count):
        return [
            pltpu.VMEM((PATHS, orders * SUB, channels), bf16),
            pltpu.VMEM((HARM, TILE, channels), f32),
            pltpu.VMEM((HARM, TILE, channels), bf16),
            pltpu.VMEM((count, subs, HARM, stack, WINDOW), bf16),
            pltpu.VMEM((count, subs, stack, WINDOW), f32),
            pltpu.VMEM((count, subs, stack, WINDOW), f32),
        ]

    feat, inner_new, inner_energy, inner_force = call(
        functools.partial(inner_kernel, orders=orders),
        "inner",
        (
            HELD((atom_rows, feature_cols), bf16),
            HELD((inner, TILE, channels), bf16),
            HELD((inner, 1, TILE), f32),
            HELD((8, atom_rows), f32),
        ),
        [pltpu.VMEM((feature_cols, atom_rows), bf16), pltpu.VMEM((atom_rows, 8), f32)]
        + scratch(inner)
        + [pltpu.SemaphoreType.DMA((inner, subs)), pltpu.SemaphoreType.DMA((inner, 2))],
        inner * tile_flops,
        arrival_live,
        received,
        rows,
        distant(edges),
        distant(values),
        distant(changes),
        gains,
        *common,
        distant=(3, 4, 5),
    )
    new_rows, energies, forces = call(
        functools.partial(outer_kernel, orders=orders),
        "outer",
        (
            shape((atom_rows, channels), bf16),
            shape((1, atom_rows), f32),
            shape((8, atom_rows), f32),
        ),
        [
            pltpu.VMEM((4 * TILE, feature_cols), bf16),
            pltpu.VMEM((feature_cols, 4 * TILE), bf16),
            pltpu.VMEM((8, 4 * TILE), f32),
            pltpu.VMEM((4 * TILE, 8), f32),
        ]
        + scratch(2)
        + [pltpu.VMEM((2, 8, WINDOW), f32)],
        2 * tile_flops,
        low,
        high,
        held(feat),
        low_rows,
        rows,
        high_rows,
        table,
        *common,
        held(inner_new),
        held(inner_energy),
        held(inner_force),
    )
    return (energies.reshape(atom_rows), forces[:3].T, new_rows)


def solution(mesh):
    placed = (
        P(("dom", "blk"), None),
        P(("dom", "blk")),
        P(("dom", "blk"), None),
        P(("dom", "blk")),
        P(("dom", "blk")),
        P(("dom", "blk"), None),
        P(),
        P(),
        P(),
        P(),
        P(),
    )
    return jax.shard_map(
        per_device,
        mesh=mesh,
        in_specs=placed,
        out_specs=(P(("dom", "blk")), P(("dom", "blk"), None), P(("dom", "blk"), None)),
        check_vma=False,
    )
```

time: 522 us -> 106 us (0.20); the launches traced: 514 us -> 105 us
  other arithmetic: 198 us -> 0.69 us
  matrix products: 162 us -> 0.68 us
  local copies, waits for them, and re-layouts: 95.3 us -> 1.33 us
  Pallas kernels: 0 us -> 61.9 us
  loops' own time: 7.81 us -> 0 us
  starting transfers between devices: 25.8 us -> 19 us
    dot_general x133 -> x1, matrix products: 162 us -> 0.68 us  [per_device(): gains = jnp.dot(one_hot, table, precision=lax.Precision.HIGHEST)]
    pallas_call x0 -> x4, Pallas kernels: none -> 61.9 us  [the longest x3 49.4 us: call(): pl.pallas_call(kernel, out_shape=out_shape, in_specs=[hbm if at in distan...]
    reduce_sum x72 -> x0, other arithmetic: 47.2 us -> none  [the longest x12 26.3 us: edge_factors(): radial = envelope[None] * jnp.cos(orders[:, None, None] * spread[None])]
    mul x60 -> x0, other arithmetic: 32.5 us -> none  [the longest x12 21 us: edge_factors(): radial = envelope[None] * jnp.cos(orders[:, None, None] * spread[None])]
    while x708 -> x0, local copies, waits for them, and re-layouts: 29 us -> none
    convert_element_type x49 -> x3, other arithmetic: 28.6 us -> 0.08 us  [the longest x1 0.07 us: per_device(): live.astype(f32)]
    dynamic_update_slice x24 -> x0, other arithmetic: 25.6 us -> none  [the longest x12 17.4 us: one_block(): energies = lax.dynamic_update_slice_in_dim(energies, energy, start_row, 0)]
    select_n x14 -> x1, other arithmetic: 23.5 us -> 0.01 us  [per_device(): arrival_live = jnp.where(live, arrival.reshape(1, atom_rows), -1)]
  transfers between devices with their start and end apart: 7 -> 5, of which waited for: 2 -> 1; matrix products, arithmetic and copies ran while one was open for 4% -> 1% of each run, Pallas kernels for 0% -> 45%
where the time goes in v2:
time: 106 us; the launch traced here: 105 us
  Pallas kernels  61.9 us (58%)
  waiting for transfers between devices  20.9 us (20%)
  starting transfers between devices  19 us (18%)
  local copies, waits for them, and re-layouts  1.33 us (1%)
    pallas_call x3, Pallas kernels, call(): pl.pallas_call(kernel, out_shape=out_shape, in_specs=[hbm if at in distan...  49.4 us
    all_to_all x1, waiting for transfers between devices, per_device(): lax.all_to_all(parcels, AXES, split_axis=0, concat_axis=0, tiled=True)  20.9 us
    pallas_call x1, Pallas kernels, per_device(): pl.pallas_call(functools.partial(pairs_kernel, orders=orders), grid=(inne...  12.5 us
    ppermute x2, starting transfers between devices, from_sides(): high = lax.ppermute(block_low, AXES, backward)  8.95 us
    all_to_all x1, starting transfers between devices, per_device(): lax.all_to_all(parcels, AXES, split_axis=0, concat_axis=0, tiled=True)  6.1 us
    ppermute x2, starting transfers between devices, from_sides(): low = lax.ppermute(block_high, AXES, forward)  3.98 us
  transfers between devices with their start and end apart: 5, of which 1 were waited for; matrix products, arithmetic and copies ran while one was open for 1% of the time, Pallas kernels for 45%

profile of v2, /device:TPU:4, one launch (start us, length us, event | category | flops | bytes accessed | tf_op | source)
XLA Modules:
  0.0 105.4 jit_solution(6367986724459380145)
XLA Ops:
  0.6 0.0 copy-start.8
  0.6 0.0 copy-start.9
  0.7 6.1 %all-to-all-start = ((bf16[32,24,1152]{2,1,0:T(8,128)(2,1)}), bf16[32,24,1152]{2,1,0:T(8,128)(2,1)S(1)}, u32[]{:S(2)}, u32[]{:S(2)}) async-start(bf16[32,24,1152]{2,1,0:T(8,128)(2,1)} %bitcast.20), calls=%async_computation | async-start | bytes 3538944 | tf_op jit(solution)/shard_map/all_to_all | solution.py:505
  6.8 0.1 broadcast_in_dim.27
  6.9 0.1 reshape.72
  7.0 0.1 broadcast_in_dim.29
  7.1 0.1 reshape.73
  7.2 0.1 fusion.2
  7.2 0.1 reshape.78
  7.3 0.0 copy-done.6
  7.4 2.1 %collective-permute-start.2 = (f32[8,128]{1,0:T(8,128)S(1)}, f32[8,128]{1,0:T(8,128)S(1)}, u32[]{:S(2)}, u32[]{:S(2)}) collective-permute-start(f32[8,128]{1,0:T(8,128)S(1)} %get-tuple-element.28), channel_id=1, source_target_pairs={{0,1},{1,2},{2,3},{3,4},{4,5},{5,6},{6,7},{7,8},{8,9},{9,10},{10,1... | collective-permute-start | bytes 12296 | tf_op jit(solution)/shard_map/ppermute | solution.py:483
  9.5 4.4 %collective-permute-start.3 = (f32[8,128]{1,0:T(8,128)S(1)}, f32[8,128]{1,0:T(8,128)S(1)}, u32[]{:S(2)}, u32[]{:S(2)}) collective-permute-start(f32[8,128]{1,0:T(8,128)S(1)} %get-tuple-element.27), channel_id=1, source_target_pairs={{1,0},{2,1},{3,2},{4,3},{5,4},{6,5},{7,6},{8,7},{9,8},{10,9},{11,1... | collective-permute-start | bytes 12296 | tf_op jit(solution)/shard_map/ppermute | solution.py:484
  13.9 0.1 lt.29
  14.0 0.0 copy-done.7
  14.0 0.1 copy.16
  14.2 0.7 fusion.gains_ref
  14.9 12.5 %pairs.1 = (bf16[5,4,9,256,256]{4,3,2,1,0:T(8,128)(2,1)}, f32[5,4,256,256]{3,2,1,0:T(8,128)}, f32[5,4,256,256]{3,2,1,0:T(8,128)}) custom-call(f32[8,768]{1,0:T(8,128)S(1)} %concatenate.3.rows_ref), custom_call_target="tpu_custom_call" | custom-call | flops 10000000000 | bytes 41943040 | tf_op jit(solution)/shard_map/pairs/pallas_call | solution.py:538
  27.4 20.9 %all-to-all-done = bf16[32,24,1152]{2,1,0:T(8,128)(2,1)S(1)} async-done(((bf16[32,24,1152]{2,1,0:T(8,128)(2,1)}), bf16[32,24,1152]{2,1,0:T(8,128)(2,1)S(1)}, u32[]{:S(2)}, u32[]{:S(2)}) %all-to-all-start) | async-done | bytes 1769504 | tf_op jit(solution)/shard_map/all_to_all | solution.py:505
  48.2 0.9 edge_tiles.1
  49.1 1.9 %collective-permute-start = (bf16[128,1152]{1,0:T(8,128)(2,1)S(1)}, bf16[128,1152]{1,0:T(8,128)(2,1)S(1)}, u32[]{:S(2)}, u32[]{:S(2)}) collective-permute-start(bf16[128,1152]{1,0:T(8,128)(2,1)S(1)} %get-tuple-element.15), channel_id=1, source_target_pairs={{0,1},{1,2},{2,3},{3,4},{4,5},{5,6},{6,7},{7,8},{8,9},{9,10},{10,1... | collective-permute-start | bytes 884744 | tf_op jit(solution)/shard_map/ppermute | solution.py:483
  51.0 4.5 %collective-permute-start.1 = (bf16[128,1152]{1,0:T(8,128)(2,1)S(1)}, bf16[128,1152]{1,0:T(8,128)(2,1)S(1)}, u32[]{:S(2)}, u32[]{:S(2)}) collective-permute-start(bf16[128,1152]{1,0:T(8,128)(2,1)S(1)} %get-tuple-element.16), channel_id=1, source_target_pairs={{1,0},{2,1},{3,2},{4,3},{5,4},{6,5},{7,6},{8,7},{9,8},{10,9},{11,1... | collective-permute-start | bytes 884744 | tf_op jit(solution)/shard_map/ppermute | solution.py:484
  55.5 0.0 copy-done
  55.6 0.0 copy-done.1
  55.6 0.0 copy-done.2
  55.6 34.2 %inner.1 = (bf16[768,1152]{1,0:T(8,128)(2,1)S(1)}, bf16[5,128,128]{2,1,0:T(8,128)(2,1)S(1)}, f32[5,1,128]{2,1,0:T(1,128)S(1)}, f32[8,768]{1,0:T(8,128)S(1)}) custom-call(s32[1,768]{1,0:T(1,128)S(1)} %select_n.7.arrival_ref, bf16[768,1152]{1,0:T(8,128)(2,1)S(1)} %bitcast.15, f32[8,768]{1,0:T(8,128)S(1)} %concatenate.3.rows_ref, ...), custom_call_target="tpu_custom_call" | custom-call | flops 16777216000 | bytes 4194304 | tf_op jit(solution)/shard_map/inner/pallas_call | solution.py:467
  89.8 0.0 collective-permute-done.2.low_rows_ref
  89.8 0.0 collective-permute-done.3.high_rows_ref
  89.8 0.0 collective-permute-done.low_ref
  89.9 0.0 collective-permute-done.1.high_ref
  89.9 14.3 %outer.1 = (bf16[768,128]{1,0:T(8,128)(2,1)}, f32[1,768]{1,0:T(1,128)S(1)}, f32[8,768]{1,0:T(8,128)S(1)}) custom-call(bf16[128,1152]{1,0:T(8,128)(2,1)S(1)} %collective-permute-done.low_ref, bf16[128,1152]{1,0:T(8,128)(2,1)S(1)} %collective-permute-done.1.high_ref, bf16[768,1152]{1,0:T(8,128)(2,1)S(1)} %get-tuple-element.20.feat_ref, ...), custom_call_target="tpu_custom_call" | custom-call | flops 6710886400 | bytes 4194304 | tf_op jit(solution)/shard_map/outer/pallas_call | solution.py:467
  104.2 0.6 slice_bitcast_fusion
  104.8 0.6 reduce
  (26 shorter events, 0.2 us)
Async XLA Ops:
  0.6 6.2 %copy-start.8 = (s32[12,3]{0,1:T(4,128)S(1)}, s32[12,3]{0,1:T(4,128)}, u32[]{:S(2)}) copy-start(s32[12,3]{0,1:T(4,128)} %param.16) | copy-start | bytes 436
  0.6 6.5 %copy-start.9 = (s32[12]{0:T(128)S(1)}, s32[12]{0:T(128)}, u32[]{:S(2)}) copy-start(s32[12]{0:T(128)} %param.15) | copy-start | bytes 148
  0.7 6.7 %copy-start.5 = (s32[768]{0:T(1024)S(1)}, s32[768]{0:T(1024)}, u32[]{:S(2)}) copy-start(s32[768]{0:T(1024)} %param.14) | copy-start | bytes 9220
  0.7 6.7 %copy-start.6 = (f32[768,3]{0,1:T(4,128)S(1)}, f32[768,3]{0,1:T(4,128)}, u32[]{:S(2)}) copy-start(f32[768,3]{0,1:T(4,128)} %param.13) | copy-start | bytes 27652
  0.7 13.3 %copy-start.7 = (s32[768]{0:T(1024)S(1)}, s32[768]{0:T(1024)}, u32[]{:S(2)}) copy-start(s32[768]{0:T(1024)} %param.12) | copy-start | bytes 9220
  0.7 13.3 %copy-start.3 = (f32[89,3,128]{2,0,1:T(8,128)S(1)}, f32[89,3,128]{2,0,1:T(8,128)}, u32[]{:S(2)}) copy-start(f32[89,3,128]{2,0,1:T(8,128)} %param.18) | copy-start | bytes 410116
  0.7 13.5 %copy-start.4 = (f32[8,7,128]{2,0,1:T(8,128)S(1)}, f32[8,7,128]{2,0,1:T(8,128)}, u32[]{:S(2)}) copy-start(f32[8,7,128]{2,0,1:T(8,128)} %param.17) | copy-start | bytes 86020
  0.7 47.5 %all-to-all-start = ((bf16[32,24,1152]{2,1,0:T(8,128)(2,1)}), bf16[32,24,1152]{2,1,0:T(8,128)(2,1)S(1)}, u32[]{:S(2)}, u32[]{:S(2)}) async-start(bf16[32,24,1152]{2,1,0:T(8,128)(2,1)} %bitcast.20), calls=%async_computation | async-start | bytes 3538944 | tf_op jit(solution)/shard_map/all_to_all | solution.py:505
  7.4 82.4 %collective-permute-start.2 = (f32[8,128]{1,0:T(8,128)S(1)}, f32[8,128]{1,0:T(8,128)S(1)}, u32[]{:S(2)}, u32[]{:S(2)}) collective-permute-start(f32[8,128]{1,0:T(8,128)S(1)} %get-tuple-element.28), channel_id=1, source_target_pairs={{0,1},{1,2},{2,3},{3,4},{4,5},{5,6},{6,7},{7,8},{8,9},{9,10},{10,1... | collective-permute-start | bytes 12296 | tf_op jit(solution)/shard_map/ppermute | solution.py:483
  9.5 80.4 %collective-permute-start.3 = (f32[8,128]{1,0:T(8,128)S(1)}, f32[8,128]{1,0:T(8,128)S(1)}, u32[]{:S(2)}, u32[]{:S(2)}) collective-permute-start(f32[8,128]{1,0:T(8,128)S(1)} %get-tuple-element.27), channel_id=1, source_target_pairs={{1,0},{2,1},{3,2},{4,3},{5,4},{6,5},{7,6},{8,7},{9,8},{10,9},{11,1... | collective-permute-start | bytes 12296 | tf_op jit(solution)/shard_map/ppermute | solution.py:484
  27.3 28.2 %copy-start = (bf16[128,128]{1,0:T(8,128)(2,1)S(1)}, bf16[128,128]{1,0:T(8,128)(2,1)}, u32[]{:S(2)}) copy-start(bf16[128,128]{1,0:T(8,128)(2,1)} %mix_ref.3) | copy-start | bytes 98308
  27.3 28.2 %copy-start.1 = (bf16[128,128]{1,0:T(8,128)(2,1)S(1)}, bf16[128,128]{1,0:T(8,128)(2,1)}, u32[]{:S(2)}) copy-start(bf16[128,128]{1,0:T(8,128)(2,1)} %self_ref.3) | copy-start | bytes 98308
  27.3 28.2 %copy-start.2 = (f32[128]{0:T(128)S(1)}, f32[128]{0:T(128)}, u32[]{:S(2)}) copy-start(f32[128]{0:T(128)} %param.21) | copy-start | bytes 1540
  49.1 40.8 %collective-permute-start = (bf16[128,1152]{1,0:T(8,128)(2,1)S(1)}, bf16[128,1152]{1,0:T(8,128)(2,1)S(1)}, u32[]{:S(2)}, u32[]{:S(2)}) collective-permute-start(bf16[128,1152]{1,0:T(8,128)(2,1)S(1)} %get-tuple-element.15), channel_id=1, source_target_pairs={{0,1},{1,2},{2,3},{3,4},{4,5},{5,6},{6,7},{7,8},{8,9},{9,10},{10,1... | collective-permute-start | bytes 884744 | tf_op jit(solution)/shard_map/ppermute | solution.py:483
  51.0 38.9 %collective-permute-start.1 = (bf16[128,1152]{1,0:T(8,128)(2,1)S(1)}, bf16[128,1152]{1,0:T(8,128)(2,1)S(1)}, u32[]{:S(2)}, u32[]{:S(2)}) collective-permute-start(bf16[128,1152]{1,0:T(8,128)(2,1)S(1)} %get-tuple-element.16), channel_id=1, source_target_pairs={{1,0},{2,1},{3,2},{4,3},{5,4},{6,5},{7,6},{8,7},{9,8},{10,9},{11,1... | collective-permute-start | bytes 884744 | tf_op jit(solution)/shard_map/ppermute | solution.py:484
